TPU v7x, 256 devices: a whole 4x4x8 slice. The times are simulated.
256 devices in a mesh: ctx: 32 (over y, z_hi, core), exp: 8 (over z_lo, x).
Axes of the slice: x: 4, y: 4, z: 8 (z_hi: 4, z_lo: 2; z = z_hi * 2 + z_lo), core: 2. Of those that a mesh axis runs over, the one named last changes fastest.
Arguments:
- residual: bfloat16 [4096, 2048], P(('ctx', 'exp')), may hold values from -11 to 11
- query_states: bfloat16 [4096, 2048], P('ctx', 'exp'), may hold values from -14 to 14
- key_states: bfloat16 [4096, 2048], P('ctx', 'exp'), may hold values from -14 to 14
- value_states: bfloat16 [4096, 2048], P('ctx', 'exp'), may hold values from -6 to 6
- out_weight: bfloat16 [2048, 2048], P('exp'), may hold values from -0.125 to 0.125
- norm_gain: float32 [2048], replicated, may hold values from 0.25 to 1.75
- expert_ids: int32 [4096, 2], P(('ctx', 'exp')), may hold values from 0 to 15, all different within a row
- gate_weights: float32 [4096, 2], P(('ctx', 'exp')), may hold values from 0.2 to 1
- gate_matrix: bfloat16 [16, 2048, 6400], P('exp', None, 'ctx'), may hold values from -0.125 to 0.125
- up_matrix: bfloat16 [16, 2048, 6400], P('exp', None, 'ctx'), may hold values from -0.125 to 0.125
- down_matrix: bfloat16 [16, 6400, 2048], P('exp', 'ctx'), may hold values from -0.078125 to 0.078125
- grad_out: bfloat16 [4096, 2048], P(('ctx', 'exp')), may hold values from -6 to 6
Outputs:
- layer_out: bfloat16 [4096, 2048], P(('ctx', 'exp'))
- grad_residual: bfloat16 [4096, 2048], P(('ctx', 'exp'))
- grad_query: bfloat16 [4096, 2048], P('ctx', 'exp')
- grad_keys: bfloat16 [4096, 2048], P('ctx', 'exp')
- grad_values: bfloat16 [4096, 2048], P('ctx', 'exp')
Inputs may be any that keep to these rules, and one draw needn't show every extreme that they name: `expert_ids`: each row names 2 different experts.
All inputs are finite; a program needn't handle non-finite values.
Results may differ from a plain program's by a relative error of at most 0.04.
Values may be sent and summed in bfloat16 or wider, within the bound.
A program may use at most 128 MiB of HBM per device.

v0:
```python
import math

import jax
import jax.numpy as jnp
from jax import lax
from jax.sharding import PartitionSpec as P

HD = 128
E = 16
TOP = 2


EPSILON = 1e-05
MASKED = -1e30


def head_scores(query_part, key_part, scale_factor, allowed):
    scores = (
        jnp.einsum("qhd,khd->hqk", query_part, key_part, preferred_element_type=jnp.float32)
        * scale_factor
    )
    return jnp.where(allowed[None, :, :], scores, MASKED)


def local(
    residual,
    query_states,
    key_states,
    value_states,
    out_weight,
    norm_gain,
    expert_ids,
    gate_weights,
    gate_matrix,
    up_matrix,
    down_matrix,
    grad_out,
):
    scale_factor = 1.0 / math.sqrt(HD)
    slab_rows = query_states.shape[0]
    head_width = query_states.shape[1]
    heads_here = head_width // HD
    own_rows = residual.shape[0]
    model_width = residual.shape[1]
    hidden_here = gate_matrix.shape[2]
    capacity = own_rows * TOP // E
    slab_start = lax.axis_index("ctx") * slab_rows
    whole_keys, whole_values = (
        lax.all_gather(key_states, "ctx", axis=0, tiled=True),
        lax.all_gather(value_states, "ctx", axis=0, tiled=True),
    )
    total_rows = whole_keys.shape[0]
    query_heads = query_states.reshape(slab_rows, heads_here, HD)
    key_heads = whole_keys.reshape(total_rows, heads_here, HD)
    value_heads = whole_values.reshape(total_rows, heads_here, HD)
    query_index = slab_start + lax.iota(jnp.int32, slab_rows)
    key_index = lax.iota(jnp.int32, total_rows)
    allowed = key_index[None, :] <= query_index[:, None]
    scores = head_scores(query_heads, key_heads, scale_factor, allowed)
    row_max = jnp.max(scores, axis=2, keepdims=True)
    log_total = row_max + jnp.log(jnp.sum(jnp.exp(scores - row_max), axis=2, keepdims=True))
    softmax = jnp.exp(scores - log_total)
    softmax_low = softmax.astype(jnp.bfloat16)
    attended = jnp.einsum(
        "hqk,khd->qhd", softmax_low, value_heads, preferred_element_type=jnp.float32
    ).astype(jnp.bfloat16)
    attended_rows = attended.reshape(slab_rows, head_width)
    projected = lax.psum_scatter(
        jnp.dot(attended_rows, out_weight, preferred_element_type=jnp.float32).astype(jnp.bfloat16),
        "exp",
        scatter_dimension=0,
        tiled=True,
    ).astype(jnp.float32)
    hidden_state = (residual.astype(jnp.float32) + projected).astype(jnp.bfloat16)
    hidden_wide = hidden_state.astype(jnp.float32)
    inverse_norm = lax.rsqrt(jnp.mean(hidden_wide * hidden_wide, axis=1, keepdims=True) + EPSILON)
    normed = (hidden_wide * inverse_norm * norm_gain).astype(jnp.bfloat16)
    flat_experts = expert_ids.reshape(own_rows * TOP)
    expert_range = lax.iota(jnp.int32, E)
    chosen = (flat_experts[:, None] == expert_range[None, :]).astype(jnp.int32)
    earlier = jnp.cumsum(chosen, axis=0, dtype=jnp.int32) - chosen
    rank_index = jnp.sum(earlier * chosen, axis=1, dtype=jnp.int32)
    slot_index = rank_index * E + flat_experts
    slot_table = (slot_index[:, None] == lax.iota(jnp.int32, capacity * E)[None, :]).astype(
        jnp.bfloat16
    )
    weighted = (gate_weights[:, :, None] * grad_out.astype(jnp.float32)[:, None, :]).astype(
        jnp.bfloat16
    )
    outgoing = jnp.concatenate(
        (jnp.repeat(normed, TOP, axis=0), weighted.reshape(own_rows * TOP, model_width)), axis=1
    )
    dispatched = jnp.einsum(
        "js,jd->sd", slot_table, outgoing, preferred_element_type=jnp.float32
    ).astype(jnp.bfloat16)
    arrived = lax.all_to_all(
        dispatched.reshape(capacity, E, 2 * model_width),
        "exp",
        split_axis=1,
        concat_axis=0,
        tiled=True,
    )
    shard_piece = lax.all_gather(arrived, "ctx", axis=0, tiled=True)
    inputs_part = shard_piece[:, :, :model_width]
    grads_part = shard_piece[:, :, model_width:]
    gate_part = jnp.einsum(
        "sed,edf->sef", inputs_part, gate_matrix, preferred_element_type=jnp.float32
    )
    up_part = jnp.einsum("sed,edf->sef", inputs_part, up_matrix, preferred_element_type=jnp.float32)
    sigmoid_part = jax.nn.sigmoid(gate_part)
    active = (gate_part * sigmoid_part * up_part).astype(jnp.bfloat16)
    grad_active = jnp.einsum(
        "sed,efd->sef", grads_part, down_matrix, preferred_element_type=jnp.float32
    )
    grad_gate = (
        grad_active * up_part * sigmoid_part * (1.0 + gate_part * (1.0 - sigmoid_part))
    ).astype(jnp.bfloat16)
    grad_up = (grad_active * gate_part * sigmoid_part).astype(jnp.bfloat16)
    unit_terms = jnp.concatenate((active, grad_gate, grad_up), axis=2)
    active = unit_terms[:, :, :hidden_here]
    grad_gate = unit_terms[:, :, hidden_here : 2 * hidden_here]
    grad_up = unit_terms[:, :, 2 * hidden_here :]
    out_term = jnp.einsum("sef,efd->sed", active, down_matrix, preferred_element_type=jnp.float32)
    grad_term = jnp.einsum(
        "sef,edf->sed", grad_gate, gate_matrix, preferred_element_type=jnp.float32
    ) + jnp.einsum("sef,edf->sed", grad_up, up_matrix, preferred_element_type=jnp.float32)
    summed = lax.psum_scatter(
        jnp.concatenate((out_term, grad_term), axis=2).astype(jnp.bfloat16),
        "ctx",
        scatter_dimension=0,
        tiled=True,
    )
    returned = lax.all_to_all(summed, "exp", split_axis=0, concat_axis=1, tiled=True)
    picked = jnp.dot(
        slot_table,
        returned.reshape(capacity * E, 2 * model_width),
        preferred_element_type=jnp.float32,
    )
    picked = picked.reshape(own_rows, TOP, 2 * model_width)
    mixture = jnp.sum(gate_weights[:, :, None] * picked[:, :, :model_width], axis=1)
    layer_out = (hidden_wide + mixture).astype(jnp.bfloat16)
    grad_normed = jnp.sum(picked[:, :, model_width:], axis=1)
    scaled_grad = norm_gain * grad_normed
    inverse_cube = inverse_norm * inverse_norm * inverse_norm
    grad_hidden = grad_out.astype(jnp.float32) + (
        inverse_norm * scaled_grad
        - hidden_wide * inverse_cube * jnp.mean(hidden_wide * scaled_grad, axis=1, keepdims=True)
    )
    grad_residual = grad_hidden.astype(jnp.bfloat16)
    grad_attended = jnp.einsum(
        "td,fd->tf",
        lax.all_gather(grad_residual, "exp", axis=0, tiled=True),
        out_weight,
        preferred_element_type=jnp.float32,
    ).astype(jnp.bfloat16)
    grad_heads = grad_attended.reshape(slab_rows, heads_here, HD)
    row_delta = jnp.sum(grad_heads.astype(jnp.float32) * attended.astype(jnp.float32), axis=2)
    grad_prob = jnp.einsum(
        "qhd,khd->hqk", grad_heads, value_heads, preferred_element_type=jnp.float32
    )
    grad_score = (softmax * (grad_prob - row_delta.T[:, :, None])).astype(jnp.bfloat16)
    grad_query = (
        (
            jnp.einsum("hqk,khd->qhd", grad_score, key_heads, preferred_element_type=jnp.float32)
            * scale_factor
        )
        .astype(jnp.bfloat16)
        .reshape(slab_rows, head_width)
    )
    key_term = jnp.einsum(
        "hqk,qhd->khd", grad_score, query_heads, preferred_element_type=jnp.float32
    )
    value_term = jnp.einsum(
        "hqk,qhd->khd", softmax_low, grad_heads, preferred_element_type=jnp.float32
    )
    key_sums = lax.psum_scatter(
        jnp.concatenate(
            (
                key_term.reshape(slab_rows * lax.axis_size("ctx"), head_width),
                value_term.reshape(slab_rows * lax.axis_size("ctx"), head_width),
            ),
            axis=1,
        ).astype(jnp.bfloat16),
        "ctx",
        scatter_dimension=0,
        tiled=True,
    ).astype(jnp.float32)
    grad_keys = (key_sums[:, :head_width] * scale_factor).astype(jnp.bfloat16)
    grad_values = key_sums[:, head_width:].astype(jnp.bfloat16)
    return (layer_out, grad_residual, grad_query, grad_keys, grad_values)


def solution(mesh):
    in_specs = (
        P(("ctx", "exp"), None),
        P("ctx", "exp"),
        P("ctx", "exp"),
        P("ctx", "exp"),
        P("exp", None),
        P(),
        P(("ctx", "exp"), None),
        P(("ctx", "exp"), None),
        P("exp", None, "ctx"),
        P("exp", None, "ctx"),
        P("exp", "ctx", None),
        P(("ctx", "exp"), None),
    )
    out_specs = (
        P(("ctx", "exp"), None),
        P(("ctx", "exp"), None),
        P("ctx", "exp"),
        P("ctx", "exp"),
        P("ctx", "exp"),
    )
    return jax.shard_map(local, mesh=mesh, in_specs=in_specs, out_specs=out_specs, check_vma=False)
```

profile of v0, /device:TPU:1, one launch (start us, length us, event | category | flops | bytes accessed | tf_op | source)
XLA Modules:
  0.0 581.5 jit_solution(10870940880646763430)
XLA Ops:
  7.2 1.7 copy.69
  9.0 0.7 all-gather.6.cloned.1.call-update
  9.7 1.0 copy.90
  10.7 0.4 iota_compare_fusion
  11.1 60.2 %all-gather.4.cloned.1.call-done = bf16[4096,256]{0,1:T(8,128)(2,1)} async-done(((bf16[128,256]{0,1:T(8,128)(2,1)}), bf16[4096,256]{0,1:T(8,128)(2,1)}) %all-gather.4.cloned.1.call-update) | async-done | bytes 2097168 | tf_op jit(solution)/shard_map/all_gather | solution.py:49
  71.3 2.9 fusion.51
  74.1 2.0 copy-done.2
  76.1 0.7 exponential_reduce_fusion
  76.8 49.2 %all-gather.6.cloned.1.call-done = bf16[4096,256]{1,0:T(8,128)(2,1)} async-done(((bf16[128,256]{1,0:T(8,128)(2,1)}), bf16[4096,256]{1,0:T(8,128)(2,1)}) %all-gather.6.cloned.1.call-update) | async-done | bytes 2097168 | tf_op jit(solution)/shard_map/all_gather | solution.py:50
  126.0 4.1 copy.72
  130.2 3.7 convolution_convert_fusion.5
  133.9 1.1 convolution_convert_fusion.3
  136.2 30.8 %reduce-scatter.4.cloned.1.call-done = bf16[16,2048]{1,0:T(8,128)(2,1)} async-done(((bf16[128,2048]{1,0:T(8,128)(2,1)}), bf16[16,2048]{1,0:T(8,128)(2,1)}) %reduce-scatter.4.cloned.1.call-update) | async-done | bytes 65552 | tf_op jit(solution)/shard_map/reduce_scatter | solution.py:68
  167.0 1.0 fusion.31
  168.2 0.3 convolution_convert_fusion.2
  168.6 0.3 copy.76
  168.9 8.5 %all_to_all.33 = bf16[2,16,4096]{2,0,1:T(2,128)(2,1)S(1)} all-to-all(bf16[2,16,4096]{2,0,1:T(2,128)(2,1)S(1)} %copy.76), channel_id=1, replica_groups=mesh['ctx'=32,'exp'=8] {'exp'}, dimensions={1} | all-to-all | bytes 524288 | tf_op jit(solution)/shard_map/all_to_all | solution.py:96
  177.3 0.2 copy.94
  177.5 0.8 all_to_all.27
  178.4 0.2 reduce-scatter.6.cloned.1.call-start
  178.6 81.0 %all-gather.8.cloned.1.call-done = bf16[512,2,4096]{2,0,1:T(8,128)(2,1)} async-done(((bf16[16,2,4096]{2,0,1:T(8,128)(2,1)}), bf16[512,2,4096]{2,0,1:T(8,128)(2,1)}) %all-gather.8.cloned.1.call-update) | async-done | bytes 8388624 | tf_op jit(solution)/shard_map/all_gather | solution.py:103
  259.7 4.3 fusion.11
  264.0 3.9 fusion.14
  267.9 3.3 convert_bitcast_fusion
  271.2 1.5 fusion.17
  272.7 1.5 fusion.23
  274.2 3.4 fusion.10
  277.6 7.8 %pad_maximum_fusion = bf16[512,2,4096]{2,0,1:T(8,128)(2,1)} fusion(bf16[512,2,2048]{2,0,1:T(8,128)(2,1)} %fusion.10, bf16[512,2,2048]{2,0,1:T(8,128)(2,1)} %convert_bitcast_fusion), kind=kLoop, calls=%fused_computation | loop fusion | flops 16777216 | bytes 16777216 | tf_op jit(solution)/shard_map/concatenate | solution.py:128
  285.5 121.1 %reduce-scatter.6.cloned.1.call-done = bf16[16,2,4096]{2,0,1:T(8,128)(2,1)} async-done(((bf16[512,2,4096]{2,0,1:T(8,128)(2,1)}), bf16[16,2,4096]{2,0,1:T(8,128)(2,1)}) %reduce-scatter.6.cloned.1.call-update) | async-done | bytes 262160 | tf_op jit(solution)/shard_map/reduce_scatter | solution.py:127
  406.6 1.9 copy.78
  408.5 4.1 all-to-all-start.1
  412.8 5.9 %all-to-all-done.1 = bf16[16,2,4096]{2,1,0:T(2,128)(2,1)S(1)} async-done(((bf16[16,2,4096]{2,1,0:T(2,128)(2,1)}), bf16[16,2,4096]{2,1,0:T(2,128)(2,1)S(1)}, u32[]{:S(2)}, u32[]{:S(2)}) %all-to-all-start.1) | async-done | bytes 262176 | tf_op jit(solution)/shard_map/all_to_all | solution.py:133
  418.7 0.2 copy.93
  419.0 0.3 fusion.42
  419.5 0.6 fusion.38
  420.1 23.5 %all_gather.15 = bf16[128,2048]{1,0:T(8,128)(2,1)S(1)} all-gather(bf16[16,2048]{1,0:T(8,128)(2,1)S(1)} %get-tuple-element.29), channel_id=1, replica_groups=mesh['ctx'=32,'exp'=8] {'exp'}, dimensions={0}, use_global_device_ids=true | all-gather | bytes 589824 | tf_op jit(solution)/shard_map/all_gather | solution.py:152
  443.7 0.5 convolution_convert_fusion.4
  444.3 4.5 convolution_convert_fusion.1
  448.8 4.2 fusion.2
  453.0 4.1 copy.85
  457.1 3.6 convolution_convert_fusion
  460.8 4.1 copy.84
  464.8 4.5 pad_maximum_fusion.1
  469.3 3.0 fusion.20
  472.4 0.7 copy.86
  473.1 98.6 %reduce-scatter.8.cloned.1.call-done = bf16[128,512]{1,0:T(8,128)(2,1)} async-done(((bf16[4096,512]{1,0:T(8,128)(2,1)}), bf16[128,512]{1,0:T(8,128)(2,1)}) %reduce-scatter.8.cloned.1.call-update) | async-done | bytes 131088 | tf_op jit(solution)/shard_map/reduce_scatter | solution.py:176
  571.7 1.5 multiply_convert_fusion.7
  573.2 1.5 slice.34
  (66 shorter events, 2.2 us)
Async XLA Ops:
  7.2 260.7 %copy-start = (bf16[2,200,2048]{2,1,0:T(8,128)(2,1)S(1)}, bf16[2,200,2048]{2,1,0:T(8,128)(2,1)}, u32[]{:S(2)}) copy-start(bf16[2,200,2048]{2,1,0:T(8,128)(2,1)} %param.22) | copy-start | bytes 4915204
  7.2 64.1 %all-gather.4.cloned.1.call-start = ((), (), s32[]{:S(2)}) async-start(), calls=%async_computation.5 | async-start | bytes 2162688 | tf_op jit(solution)/shard_map/all_gather | solution.py:49
  8.9 117.1 %all-gather.6.cloned.1.call-start = ((), (), s32[]{:S(2)}) async-start(), calls=%async_computation.6 | async-start | bytes 2162688 | tf_op jit(solution)/shard_map/all_gather | solution.py:50
  9.7 157.3 %reduce-scatter.4.cloned.1.call-start = ((), (), s32[]{:S(2)}) async-start(), calls=%async_computation.7 | async-start | bytes 589824 | tf_op jit(solution)/shard_map/reduce_scatter | solution.py:68
  74.1 2.0 copy-start.2
  130.1 3.8 copy-start.4
  130.1 5.0 copy-start.7
  130.1 5.3 copy-start.11
  130.1 5.5 copy-start.12
  130.1 36.9 %copy-start.10 = (bf16[16,2048]{1,0:T(8,128)(2,1)S(1)}, bf16[16,2048]{1,0:T(8,128)(2,1)}, u32[]{:S(2)}) copy-start(bf16[16,2048]{1,0:T(8,128)(2,1)} %param.12) | copy-start | bytes 196612
  130.1 37.9 %copy-start.9 = (f32[2048]{0:T(1024)S(1)}, f32[2048]{0:T(1024)}, u32[]{:S(2)}) copy-start(f32[2048]{0:T(1024)} %param.17) | copy-start | bytes 24580
  135.1 124.6 %all-gather.8.cloned.1.call-start = ((), (), s32[]{:S(2)}) async-start(), calls=%async_computation.8 | async-start | bytes 8650752 | tf_op jit(solution)/shard_map/all_gather | solution.py:103
  178.4 228.2 %reduce-scatter.6.cloned.1.call-start = ((), (), s32[]{:S(2)}) async-start(), calls=%async_computation.9 | async-start | bytes 8650752 | tf_op jit(solution)/shard_map/reduce_scatter | solution.py:127
  259.7 4.4 copy-start.6
  259.7 11.5 %slice-start = ((s8[8388608]{0:T(1024)(128)(4,1)}), s8[4194304]{0:T(1024)(128)(4,1)S(1)}, s32[]{:S(2)}) async-start(s8[8388608]{0:T(1024)(128)(4,1)} %bitcast.82), calls=%async_computation.11 | async-start | bytes 8388608
  264.0 7.2 %slice-start.1 = ((s8[8388608]{0:T(1024)(128)(4,1)}), s8[4194304]{0:T(1024)(128)(4,1)S(1)}, s32[]{:S(2)}) async-start(s8[8388608]{0:T(1024)(128)(4,1)} %bitcast.82), calls=%async_computation.12 | async-start | bytes 8388608
  271.2 1.5 copy-start.5
  408.5 10.2 %all-to-all-start.1 = ((bf16[16,2,4096]{2,1,0:T(2,128)(2,1)}), bf16[16,2,4096]{2,1,0:T(2,128)(2,1)S(1)}, u32[]{:S(2)}, u32[]{:S(2)}) async-start(bf16[16,2,4096]{2,1,0:T(2,128)(2,1)} %copy.78), calls=%async_computation.3 | async-start | bytes 524288 | tf_op jit(solution)/shard_map/all_to_all | solution.py:133
  412.6 159.1 %reduce-scatter.8.cloned.1.call-start = ((), (), s32[]{:S(2)}) async-start(), calls=%async_computation.10 | async-start | bytes 4325376 | tf_op jit(solution)/shard_map/reduce_scatter | solution.py:176
  420.1 28.7 %copy-start.8 = (bf16[16,2048]{1,0:T(8,128)(2,1)}, bf16[16,2048]{1,0:T(8,128)(2,1)S(1)}, u32[]{:S(2)}) copy-start(bf16[16,2048]{1,0:T(8,128)(2,1)S(1)} %get-tuple-element.29) | copy-start | bytes 196612
  444.3 4.5 copy-start.3
  469.3 105.4 %copy-start.1 = (bf16[2,200,2048]{2,1,0:T(8,128)(2,1)S(1)}, bf16[2,200,2048]{2,1,0:T(8,128)(2,1)}, u32[]{:S(2)}) copy-start(bf16[2,200,2048]{2,1,0:T(8,128)(2,1)} %param.22) | copy-start | bytes 4915204
Sparse Core Ops, SparseCore 0:
  11.1 60.1 all-gather.3
  73.8 52.1 all-gather.5
  135.2 31.7 reduce-scatter.3
  178.5 81.1 all-gather.7
  285.6 120.9 reduce-scatter.5
  469.4 102.2 reduce-scatter.7
where the time goes:
time: 583 us; the launch traced here: 582 us
  waiting for transfers between devices  448 us (77%)
  matrix products  42 us (7%)
  blocking collectives  32 us (5%)
  local copies, waits for them, and re-layouts  23.7 us (4%)
  other arithmetic  17.2 us (3%)
  between operations  14.4 us (2%)
    reduce_scatter x1, waiting for transfers between devices, local(): lax.psum_scatter(jnp.concatenate((out_term, grad_term), axis=2).astype(jn...  121 us
    reduce_scatter x1, waiting for transfers between devices, local(): lax.psum_scatter(jnp.concatenate((key_term.reshape(slab_rows * lax.axis_s...  98.6 us
    all_gather x1, waiting for transfers between devices, local(): shard_piece = lax.all_gather(arrived, 'ctx', axis=0, tiled=True)  81 us
    all_gather x1, waiting for transfers between devices, local(): lax.all_gather(key_states, 'ctx', axis=0, tiled=True)  60.2 us
    all_gather x1, waiting for transfers between devices, local(): lax.all_gather(value_states, 'ctx', axis=0, tiled=True)  49.2 us
    reduce_scatter x1, waiting for transfers between devices, local(): lax.psum_scatter(jnp.dot(attended_rows, out_weight, preferred_element_typ...  30.8 us
    all_gather x1, blocking collectives, local(): lax.all_gather(grad_residual, 'exp', axis=0, tiled=True)  23.5 us
  transfers between devices with their start and end apart: 7, of which 7 were waited for; matrix products, arithmetic and copies ran while one was open for 2% of the time, Pallas kernels for 0%

commit v1 on v0

v1 whole, which is shorter than its diff:
```python
import functools
import math

import jax
import jax.numpy as jnp
from jax import lax
from jax.experimental import pallas as pl
from jax.experimental.pallas import tpu as pltpu
from jax.sharding import PartitionSpec as P

MESH = pl.DeviceIdType.MESH
F32 = jnp.float32
BF16 = jnp.bfloat16
HD = 128
D = 2048
ROWS = 16
CHIPS = 16
N_EXP = 8
CHIP_ROWS = 256
HIDDEN = 200
CHUNK = 1024
EPSILON = 1e-05
MASKED = -1e30
SCALE = 1.0 / math.sqrt(HD)
VMEM_LIMIT = 58 * 1024 * 1024
NT = (((1,), (1,)), ((), ()))
TN = (((0,), (0,)), ((), ()))


def rel(dy, dz):
    return dy * 4 + dz


class Net:
    def __init__(self, send, recv):
        self.send, self.recv, self.count, self.started = send, recv, 0, []
        ctx = lax.axis_index("ctx")
        self.exp = lax.axis_index("exp")
        self.core = lax.rem(ctx, 2)
        chip = ctx // 2
        self.y, self.z = chip // 4, lax.rem(chip, 4)
        at = lambda y, z, c: {"ctx": (lax.rem(y, 4) * 4 + lax.rem(z, 4)) * 2 + c}
        self.yp = at(self.y + 1, self.z, self.core)
        self.ym = at(self.y + 3, self.z, self.core)
        self.zp = at(self.y, self.z + 1, self.core)
        self.zm = at(self.y, self.z + 3, self.core)
        self.sibling = at(self.y, self.z, 1 - self.core)
        self.peers = [lax.rem(self.exp + d, N_EXP) for d in range(1, N_EXP)]

    def copy(self, src, dst, device):
        i = self.count
        self.count += 1
        made = pltpu.make_async_remote_copy(
            src_ref=src,
            dst_ref=dst,
            send_sem=self.send.at[i],
            recv_sem=self.recv.at[i],
            device_id=device,
            device_id_type=MESH,
        )
        made.start()
        self.started.append(made)
        return made

    def finish(self):
        for made in self.started:
            made.wait_send()

    def barrier(self, devices):
        sem = pltpu.get_barrier_semaphore()
        for device in devices:
            pl.semaphore_signal(sem, inc=1, device_id=device, device_id_type=MESH)
        pl.semaphore_wait(sem, len(devices))

    def ring_devices(self):
        return [self.yp, self.ym, self.zp, self.zm]

    def peer_devices(self):
        return [{"exp": peer} for peer in self.peers]

    def push(self, src_of, dst):
        return [self.copy(src_of(peer), dst, {"exp": peer}) for peer in self.peers]


def gather_steps(net, full, half, seen):
    state = {}

    def send_z():
        state["z3"] = net.copy(full(rel(0, 0)), full(rel(0, 3)), net.zp)
        state["z1"] = net.copy(full(rel(0, 0)), full(rel(0, 1)), net.zm)

    def send_y(dz):
        state["y3", dz] = net.copy(full(rel(0, dz)), full(rel(3, dz)), net.yp)
        state["y1", dz] = net.copy(full(rel(0, dz)), full(rel(1, dz)), net.ym)

    def near_z3():
        state["z3"].wait_recv()
        state["h0"] = net.copy(half(rel(0, 3), 0), half(rel(0, 2), 0), net.zp)
        send_y(3)
        seen(rel(0, 3))

    def near_z1():
        state["z1"].wait_recv()
        state["h1"] = net.copy(half(rel(0, 1), 1), half(rel(0, 2), 1), net.zm)
        send_y(1)
        seen(rel(0, 1))

    def far_z():
        state["h0"].wait_recv()
        state["h1"].wait_recv()
        send_y(2)
        seen(rel(0, 2))

    def near_y(dz):
        state["y3", dz].wait_recv()
        state["g0", dz] = net.copy(half(rel(3, dz), 0), half(rel(2, dz), 0), net.yp)
        state["y1", dz].wait_recv()
        state["g1", dz] = net.copy(half(rel(1, dz), 1), half(rel(2, dz), 1), net.ym)
        seen(rel(3, dz))
        seen(rel(1, dz))

    def far_y(dz):
        state["g0", dz].wait_recv()
        state["g1", dz].wait_recv()
        seen(rel(2, dz))

    first = [send_z, lambda: send_y(0)]
    relays = [near_z3, near_z1, lambda: near_y(0), far_z]
    relays += [lambda dz=dz: near_y(dz) for dz in (3, 1, 2)]
    last = [lambda dz=dz: far_y(dz) for dz in (0, 3, 1, 2)]
    return first, relays, last


def reduce_steps(net, full, half, near, far, load, store):
    ra, rb, za, zb = far
    rc, rd, zc, zd = near
    state = {}

    def send_far(dz):
        state["a", dz] = net.copy(half(rel(2, dz), 0), ra.at[dz], net.yp)
        state["b", dz] = net.copy(half(rel(2, dz), 1), rb.at[dz], net.ym)

    def add(target, *sources):
        total = load(target)
        for source in sources:
            total = total + load(source)
        store(target, total)

    def send_near(dz):
        state["a", dz].wait_recv()
        add(half(rel(1, dz), 0), ra.at[dz])
        state["c", dz] = net.copy(full(rel(1, dz)), rc.at[dz], net.yp)
        state["b", dz].wait_recv()
        add(half(rel(3, dz), 1), rb.at[dz])
        state["d", dz] = net.copy(full(rel(3, dz)), rd.at[dz], net.ym)

    def collect(dz):
        state["c", dz].wait_recv()
        state["d", dz].wait_recv()
        add(full(rel(0, dz)), rc.at[dz], rd.at[dz])
        if dz == 2:
            state["za"] = net.copy(half(rel(0, 2), 0), za, net.zp)
            state["zb"] = net.copy(half(rel(0, 2), 1), zb, net.zm)
        if dz == 1:
            state["za"].wait_recv()
            add(half(rel(0, 1), 0), za)
            state["zc"] = net.copy(full(rel(0, 1)), zc, net.zp)
        if dz == 3:
            state["zb"].wait_recv()
            add(half(rel(0, 3), 1), zb)
            state["zd"] = net.copy(full(rel(0, 3)), zd, net.zm)

    def last():
        state["zc"].wait_recv()
        state["zd"].wait_recv()
        add(full(rel(0, 0)), zc, zd)

    order = (2, 1, 3, 0)
    first = [lambda dz=dz: send_far(dz) for dz in order]
    rest = [lambda dz=dz: send_near(dz) for dz in order]
    rest += [lambda dz=dz: collect(dz) for dz in order]
    rest += [last]
    return first, rest


def merge(left, right):
    steps = [((i + 0.5) / len(left), 0, i) for i in range(len(left))]
    steps += [((i + 0.5) / len(right), 1, i) for i in range(len(right))]
    for _, side, i in sorted(steps):
        (left, right)[side][i]()


def load_wide(ref):
    return ref[...].astype(F32)


def store_narrow(ref, value):
    ref[...] = value.astype(BF16)


def column(ref, k):
    diagonal = lax.broadcasted_iota(jnp.int32, (ROWS, ROWS), 0) == lax.broadcasted_iota(
        jnp.int32, (ROWS, ROWS), 1
    )
    row = jnp.broadcast_to(ref[k : k + 1, :], (ROWS, ROWS))
    return jnp.sum(jnp.where(diagonal, row, jnp.zeros_like(row)), axis=1, keepdims=True)


def places(ids_ref):
    lanes = lax.broadcasted_iota(jnp.int32, (ROWS, 128), 1)
    ids = [column(ids_ref, k) for k in range(2)]
    chosen = [(lanes == one).astype(F32) for one in ids]
    lower = (
        lax.broadcasted_iota(jnp.int32, (ROWS, ROWS), 1)
        < lax.broadcasted_iota(jnp.int32, (ROWS, ROWS), 0)
    ).astype(BF16)
    earlier = jnp.dot(lower, (chosen[0] + chosen[1]).astype(BF16), preferred_element_type=F32)
    found = []
    for one, hot in zip(ids, chosen):
        rank = jnp.sum(earlier * hot, axis=1, keepdims=True).astype(jnp.int32)
        place = (one >> 1) * 16 + (one & 1) * 2 + rank
        found.append(jnp.where(rank < 2, place, -1000))
    return found


def one_hot(place, quarter):
    lanes = lax.broadcasted_iota(jnp.int32, (ROWS, 128), 1)
    return (lanes == place + 4 * quarter).astype(BF16)


def packing(quarter, transposed):
    shape, slot_dim = ((128, 32), 1) if transposed else ((32, 128), 0)
    slot = lax.broadcasted_iota(jnp.int32, shape, slot_dim)
    packed = lax.broadcasted_iota(jnp.int32, shape, 1 - slot_dim)
    want = ((slot & 15) >> 1) * 16 + quarter * 4 + (slot >> 4) * 2 + (slot & 1)
    return (packed == want).astype(BF16)


def forward_kernel(
    q_ref,
    k_ref,
    v_ref,
    ow_ref,
    residual_ref,
    gain_ref,
    ids_ref,
    gw_ref,
    go_ref,
    wg_ref,
    wu_ref,
    wd_ref,
    q_out,
    kv_out,
    p_out,
    att_out,
    hidden_out,
    arrived_out,
    wg_out,
    wu_out,
    wd_out,
    scores,
    att_pair,
    partial,
    pieces,
    packed,
    send,
    recv,
):
    net = Net(send, recv)
    core = net.core
    own_rows = pl.ds(pl.multiple_of(core * 128, 128), 128)
    own_values = pl.ds(pl.multiple_of(256 + core * 128, 128), 128)
    other_rows = pl.ds(pl.multiple_of((1 - core) * 128, 128), 128)
    net.barrier(net.ring_devices() + [net.sibling] + net.peer_devices())

    exchange = [
        net.copy(k_ref.at[:, other_rows], kv_out.at[0, own_rows, :], net.sibling),
        net.copy(v_ref.at[:, other_rows], kv_out.at[0, own_values, :], net.sibling),
        net.copy(q_ref.at[:, other_rows], q_out.at[own_rows, :], net.sibling),
    ]

    def mine(ref):
        return jnp.where(core == 0, ref[:, :128], ref[:, 128:])

    kv_out[0, own_rows, :] = mine(k_ref)
    kv_out[0, own_values, :] = mine(v_ref)
    q_out[own_rows, :] = mine(q_ref)

    chip = net.y * 4 + net.z

    def score_block(r):
        dy, dz = r // 4, r % 4
        other = lax.rem(net.y + dy, 4) * 4 + lax.rem(net.z + dz, 4)
        s = (
            lax.dot_general(q_out[...], kv_out[r, :256, :], NT, preferred_element_type=F32)
            * SCALE
        )
        row = lax.broadcasted_iota(jnp.int32, (CHIP_ROWS, CHIP_ROWS), 0) + chip * CHIP_ROWS
        column = lax.broadcasted_iota(jnp.int32, (CHIP_ROWS, CHIP_ROWS), 1) + other * CHIP_ROWS
        scores[r] = jnp.where(column <= row, s, MASKED)

    first, relays, last = gather_steps(
        net,
        lambda r: kv_out.at[r],
        lambda r, h: kv_out.at[r, pl.ds(h * 256, 256), :],
        score_block,
    )
    for made in exchange[:2]:
        made.wait_recv()
    for step in first:
        step()
    weights = [
        net.copy(wg_ref, wg_out, net.sibling),
        net.copy(wu_ref, wu_out, net.sibling),
        net.copy(wd_ref, wd_out, net.sibling),
    ]
    exchange[2].wait_recv()
    score_block(0)
    for step in relays + last:
        step()

    def top(r, m):
        s = scores[r]
        return jnp.maximum(m, jnp.maximum(s[:, :128], s[:, 128:]))

    m = lax.fori_loop(0, CHIPS, top, jnp.full((CHIP_ROWS, 128), MASKED, F32))
    m = jnp.max(m, axis=1, keepdims=True)

    def raise_all(r, total):
        e = jnp.exp(scores[r] - m)
        scores[r] = e
        return total + (e[:, :128] + e[:, 128:])

    total = lax.fori_loop(0, CHIPS, raise_all, jnp.zeros((CHIP_ROWS, 128), F32))
    inverse = 1.0 / jnp.sum(total, axis=1, keepdims=True)

    def attend(r, acc):
        low = (scores[r] * inverse).astype(BF16)
        p_out[r] = low
        return acc + jnp.dot(low, kv_out[r, 256:, :], preferred_element_type=F32)

    attended = lax.fori_loop(0, CHIPS, attend, jnp.zeros((CHIP_ROWS, HD), F32))
    att_out[...] = attended.astype(BF16)
    swap = net.copy(att_out.at[other_rows, :], att_pair.at[core], net.sibling)
    att_pair[core] = att_out[own_rows, :]
    swap.wait_recv()

    for n in range(4):
        columns = pl.ds(n * 512, 512)
        partial[:, columns] = (
            jnp.dot(att_pair[0], ow_ref[:128, columns], preferred_element_type=F32)
            + jnp.dot(att_pair[1], ow_ref[128:, columns], preferred_element_type=F32)
        ).astype(BF16)

    def piece(ref, peer):
        return ref.at[pl.ds(pl.multiple_of(peer * ROWS, ROWS), ROWS), :]

    me = net.exp
    moved = net.push(lambda peer: piece(partial, peer), piece(pieces, me))
    piece(pieces, me)[...] = piece(partial, me)[...]
    found = places(ids_ref)
    go = go_ref[...].astype(F32)
    weighted = [(column(gw_ref, k) * go).astype(BF16) for k in range(2)]
    for made in moved:
        made.wait_recv()
    projected = pieces[0:ROWS, :].astype(F32)
    for j in range(1, N_EXP):
        projected = projected + pieces[j * ROWS : (j + 1) * ROWS, :].astype(F32)
    hidden = (residual_ref[...].astype(F32) + projected).astype(BF16)
    hidden_out[...] = hidden
    wide = hidden.astype(F32)
    inverse_norm = lax.rsqrt(jnp.mean(wide * wide, axis=1, keepdims=True) + EPSILON)
    normed = (wide * inverse_norm * gain_ref[...]).astype(BF16)
    spread = jnp.zeros((128, CHUNK), F32)
    for quarter in range(4):
        for k in range(2):
            source = normed if quarter < 2 else weighted[k]
            low = (quarter % 2) * CHUNK
            spread = spread + lax.dot_general(
                one_hot(found[k], quarter),
                source[:, low : low + CHUNK],
                TN,
                preferred_element_type=F32,
            )
    packed[...] = spread.astype(BF16)
    moved = net.push(lambda peer: piece(packed, peer), piece(arrived_out, me))
    piece(arrived_out, me)[...] = piece(packed, me)[...]
    for made in moved + weights:
        made.wait_recv()
    net.finish()


def expert_kernel(
    arrived_ref,
    hidden_ref,
    gain_ref,
    ids_ref,
    gw_ref,
    go_ref,
    wg_ref,
    wu_ref,
    wd_ref,
    wg_other,
    wu_other,
    wd_other,
    layer_out,
    residual_out,
    slab_out,
    slots,
    sums,
    gates,
    ups,
    downs,
    actives,
    grad_gates,
    grad_ups,
    far_y,
    near_y,
    far_z,
    near_z,
    packed,
    returned,
    load_sem,
    send,
    recv,
):
    net = Net(send, recv)
    loads = []
    for half, sources in enumerate(((wg_ref, wu_ref, wd_ref), (wg_other, wu_other, wd_other))):
        for i, (source, target) in enumerate(zip(sources, (gates, ups, downs))):
            made = pltpu.make_async_copy(source, target.at[half], load_sem.at[half * 3 + i])
            made.start()
            loads.append(made)
    net.barrier(net.ring_devices() + net.peer_devices())

    for quarter in range(4):
        rows = jnp.dot(packing(quarter, False), arrived_ref[...], preferred_element_type=F32)
        rows = rows.astype(BF16)
        for e in range(2):
            slots[e, 0:ROWS, quarter * CHUNK : (quarter + 1) * CHUNK] = rows[e * 16 : e * 16 + 16]

    def block(ref, e):
        full = lambda r: ref.at[e, pl.ds(r * ROWS, ROWS), :]
        half = lambda r, h: ref.at[e, pl.ds(r * ROWS, ROWS), pl.ds(h * D, D)]
        return full, half

    gather = [gather_steps(net, *block(slots, e), lambda r: None) for e in range(2)]
    reduce = [
        reduce_steps(
            net,
            *block(sums, e),
            [near_y.at[e, 0], near_y.at[e, 1], near_z.at[e, 0], near_z.at[e, 1]],
            [far_y.at[e, 0], far_y.at[e, 1], far_z.at[e, 0], far_z.at[e, 1]],
            load_wide,
            store_narrow,
        )
        for e in range(2)
    ]

    def compute_steps(e):
        def enter(half):
            inputs = slots[e, :, :D]
            gate = lax.dot_general(inputs, gates[half, e], NT, preferred_element_type=F32)
            up = lax.dot_general(inputs, ups[half, e], NT, preferred_element_type=F32)
            grad = lax.dot_general(
                slots[e, :, D:], downs[half, e], NT, preferred_element_type=F32
            )
            s = jax.nn.sigmoid(gate)
            swish = gate * s
            actives[half] = (swish * up).astype(BF16)
            grad_gates[half] = (grad * up * s * (1.0 + gate * (1.0 - s))).astype(BF16)
            grad_ups[half] = (grad * swish).astype(BF16)

        def leave(n):
            columns = pl.ds(n * 512, 512)
            total = jnp.zeros((CHIP_ROWS, 512), F32)
            for half in range(2):
                total = total + jnp.dot(
                    actives[half], downs[half, e, :, columns], preferred_element_type=F32
                )
            sums[e, :, pl.ds(n * 512, 512)] = total.astype(BF16)

        def leave_grad(n):
            columns = pl.ds(n * 512, 512)
            total = jnp.zeros((CHIP_ROWS, 512), F32)
            for half in range(2):
                total = total + jnp.dot(
                    grad_gates[half], gates[half, e, :, columns], preferred_element_type=F32
                )
                total = total + jnp.dot(
                    grad_ups[half], ups[half, e, :, columns], preferred_element_type=F32
                )
            sums[e, :, pl.ds(D + n * 512, 512)] = total.astype(BF16)

        steps = [lambda half=half: enter(half) for half in range(2)]
        steps += [lambda n=n: leave(n) for n in range(4)]
        steps += [lambda n=n: leave_grad(n) for n in range(4)]
        return steps

    (first0, relays0, last0), (first1, relays1, last1) = gather
    (start0, rest0), (start1, rest1) = reduce
    for step in first0 + relays0 + first1 + last0:
        step()
    for made in loads:
        made.wait()
    merge(relays1, compute_steps(0))
    for step in start0 + last1:
        step()
    compute1 = compute_steps(1)
    merge(rest0[:4], compute1)
    for step in start1:
        step()
    merge(rest0[4:], rest1[:4])
    for step in rest1[4:]:
        step()

    def piece(ref, peer):
        return ref.at[pl.ds(pl.multiple_of(peer * ROWS, ROWS), ROWS), :]

    me = net.exp
    spread = jnp.zeros((128, CHUNK), F32)
    for quarter in range(4):
        columns = slice(quarter * CHUNK, (quarter + 1) * CHUNK)
        both = jnp.concatenate((sums[0, 0:ROWS, columns], sums[1, 0:ROWS, columns]), axis=0)
        spread = spread + jnp.dot(packing(quarter, True), both, preferred_element_type=F32)
    packed[...] = spread.astype(BF16)
    moved = net.push(lambda peer: piece(packed, peer), piece(returned, me))
    piece(returned, me)[...] = piece(packed, me)[...]
    found = places(ids_ref)
    weight = [column(gw_ref, k) for k in range(2)]
    wide = hidden_ref[...].astype(F32)
    inverse_norm = lax.rsqrt(jnp.mean(wide * wide, axis=1, keepdims=True) + EPSILON)
    for made in moved:
        made.wait_recv()

    def pick(k, quarter):
        return jnp.dot(one_hot(found[k], quarter), returned[...], preferred_element_type=F32)

    for quarter in range(2):
        columns = slice(quarter * CHUNK, (quarter + 1) * CHUNK)
        mixture = weight[0] * pick(0, quarter) + weight[1] * pick(1, quarter)
        layer_out[:, columns] = (wide[:, columns] + mixture).astype(BF16)
    grad_normed = jnp.concatenate([pick(0, q) + pick(1, q) for q in (2, 3)], axis=1)
    scaled = gain_ref[...] * grad_normed
    cube = inverse_norm * inverse_norm * inverse_norm
    grad_hidden = go_ref[...].astype(F32) + (
        inverse_norm * scaled
        - wide * cube * jnp.mean(wide * scaled, axis=1, keepdims=True)
    )
    residual_out[...] = grad_hidden.astype(BF16)
    piece(slab_out, me)[...] = residual_out[...]
    moved = net.push(lambda peer: residual_out, piece(slab_out, me))
    for made in moved:
        made.wait_recv()
    net.finish()


def backward_kernel(
    slab_ref,
    ow_ref,
    q_ref,
    kv_ref,
    p_ref,
    att_ref,
    pairs,
    grads,
    grad_heads,
    sums,
    dq_rows,
    dq_other,
    far_y,
    near_y,
    far_z,
    near_z,
    send,
    recv,
):
    net = Net(send, recv)
    core = net.core
    own_rows = pl.ds(pl.multiple_of(core * 128, 128), 128)
    other_rows = pl.ds(pl.multiple_of((1 - core) * 128, 128), 128)
    own_values = pl.ds(pl.multiple_of(256 + core * 128, 128), 128)
    other_values = pl.ds(pl.multiple_of(256 + (1 - core) * 128, 128), 128)
    net.barrier(net.ring_devices() + [net.sibling])
    for head in range(2):
        grads[head] = lax.dot_general(
            slab_ref[...], ow_ref[head * 128 : head * 128 + 128, :], NT, preferred_element_type=F32
        ).astype(BF16)
    swap = net.copy(grads.at[1 - core], grad_heads.at[own_rows, :], net.sibling)
    grad_heads[own_rows, :] = grads[core]
    swap.wait_recv()
    grad_head = grad_heads[...]
    delta = jnp.sum(grad_head.astype(F32) * att_ref[...].astype(F32), axis=1, keepdims=True)

    dq_rows[...] = jnp.zeros((CHIP_ROWS, HD), F32)

    def block(r):
        low = p_ref[r]
        grad_prob = lax.dot_general(grad_head, kv_ref[r, 256:, :], NT, preferred_element_type=F32)
        grad_score = (low.astype(F32) * (grad_prob - delta)).astype(BF16)
        dq_rows[...] += jnp.dot(grad_score, kv_ref[r, :256, :], preferred_element_type=F32)
        sums[r, :256, :] = (
            lax.dot_general(grad_score, q_ref[...], TN, preferred_element_type=F32) * SCALE
        ).astype(BF16)
        sums[r, 256:, :] = lax.dot_general(
            low, grad_head, TN, preferred_element_type=F32
        ).astype(BF16)

    start, rest = reduce_steps(
        net,
        lambda r: sums.at[r],
        lambda r, h: sums.at[r, pl.ds(h * 256, 256), :],
        [near_y.at[0], near_y.at[1], near_z.at[0], near_z.at[1]],
        [far_y.at[0], far_y.at[1], far_z.at[0], far_z.at[1]],
        load_wide,
        store_narrow,
    )
    order = (2, 1, 3, 0)
    for dz, step in zip(order, start):
        block(rel(2, dz))
        step()
    for dz, step in zip(order, rest[:4]):
        block(rel(1, dz))
        block(rel(3, dz))
        step()
    for dz in order:
        block(rel(0, dz))
    dq_other[...] = (dq_rows[other_rows, :] * SCALE).astype(BF16)
    swaps = [net.copy(dq_other, pairs.at[0, core], net.sibling)]
    pairs[0, core] = (dq_rows[own_rows, :] * SCALE).astype(BF16)
    for step in rest[4:]:
        step()
    swaps.append(net.copy(sums.at[0, other_rows, :], pairs.at[1, core], net.sibling))
    swaps.append(net.copy(sums.at[0, other_values, :], pairs.at[2, core], net.sibling))
    pairs[1, core] = sums[0, own_rows, :]
    pairs[2, core] = sums[0, own_values, :]
    for made in swaps:
        made.wait_recv()
    net.finish()


def finish_kernel(pairs, layer_ref, residual_ref, layer_out, residual_out, *outs):
    layer_out[...] = layer_ref[...]
    residual_out[...] = residual_ref[...]
    for i, out in enumerate(outs):
        out[:, :128] = pairs[i, 0]
        out[:, 128:] = pairs[i, 1]


def call(kernel, collective_id, outs, ins, scratch, copies, flops):
    shapes, out_specs = zip(*outs)
    args, in_specs = zip(*ins)
    spec = {"vmem": pl.BlockSpec(memory_space=pltpu.VMEM), "any": pl.BlockSpec(memory_space=pl.ANY)}
    return pl.pallas_call(
        kernel,
        out_shape=[jax.ShapeDtypeStruct(*shape) for shape in shapes],
        in_specs=[spec[s] for s in in_specs],
        out_specs=[spec[s] for s in out_specs],
        scratch_shapes=list(scratch)
        + [pltpu.SemaphoreType.DMA((copies,)), pltpu.SemaphoreType.DMA((copies,))],
        compiler_params=pltpu.CompilerParams(
            collective_id=collective_id, has_side_effects=True, vmem_limit_bytes=VMEM_LIMIT
        ),
        cost_estimate=pl.CostEstimate(flops=flops, bytes_accessed=1 << 24, transcendentals=0),
    )(*args)


def local(
    residual,
    query_states,
    key_states,
    value_states,
    out_weight,
    norm_gain,
    expert_ids,
    gate_weights,
    gate_matrix,
    up_matrix,
    down_matrix,
    grad_out,
):
    gain = norm_gain.reshape(1, D)
    expert_ids, gate_weights = expert_ids.T, gate_weights.T
    gate_matrix = gate_matrix.transpose(0, 2, 1)
    up_matrix = up_matrix.transpose(0, 2, 1)
    vm = lambda *args: [(arg, "vmem") for arg in args]
    hbm = lambda *args: [(arg, "any") for arg in args]
    like = lambda arg: ((arg.shape, arg.dtype), "any")
    out = lambda *shape: ((shape, BF16), "vmem")
    v = lambda *shape: pltpu.VMEM(shape, BF16)
    queries, keys_values, softmax, attended, hidden, arrived, wg, wu, wd = call(
        forward_kernel,
        0,
        [
            out(CHIP_ROWS, HD),
            out(CHIPS, 512, HD),
            out(CHIPS, CHIP_ROWS, CHIP_ROWS),
            out(CHIP_ROWS, HD),
            out(ROWS, D),
            out(128, CHUNK),
            like(gate_matrix),
            like(up_matrix),
            like(down_matrix),
        ],
        vm(
            query_states,
            key_states,
            value_states,
            out_weight,
            residual,
            gain,
            expert_ids,
            gate_weights,
            grad_out,
        )
        + hbm(gate_matrix, up_matrix, down_matrix),
        [
            pltpu.VMEM((CHIPS, CHIP_ROWS, CHIP_ROWS), F32),
            v(2, 128, HD),
            v(128, D),
            v(128, D),
            v(128, CHUNK),
        ],
        41,
        10**9,
    )
    layer_out, grad_residual, slab = call(
        expert_kernel,
        1,
        [out(ROWS, D), out(ROWS, D), out(128, D)],
        vm(arrived, hidden, gain, expert_ids, gate_weights, grad_out)
        + hbm(gate_matrix, up_matrix, down_matrix, wg, wu, wd),
        [
            v(2, CHIP_ROWS, 2 * D),
            v(2, CHIP_ROWS, 2 * D),
            v(2, 2, HIDDEN, D),
            v(2, 2, HIDDEN, D),
            v(2, 2, HIDDEN, D),
            v(2, CHIP_ROWS, HIDDEN),
            v(2, CHIP_ROWS, HIDDEN),
            v(2, CHIP_ROWS, HIDDEN),
            v(2, 2, 4, ROWS, D),
            v(2, 2, 4, ROWS, 2 * D),
            v(2, 2, ROWS, D),
            v(2, 2, ROWS, 2 * D),
            v(128, CHUNK),
            v(128, CHUNK),
            pltpu.SemaphoreType.DMA((6,)),
        ],
        94,
        5 * 10**9,
    )
    (pairs,) = call(
        backward_kernel,
        2,
        [out(3, 2, 128, HD)],
        vm(slab, out_weight, queries, keys_values, softmax, attended),
        [
            v(2, 128, HD),
            v(CHIP_ROWS, HD),
            v(CHIPS, 512, HD),
            pltpu.VMEM((CHIP_ROWS, HD), F32),
            v(128, HD),
            v(2, 4, 256, HD),
            v(2, 4, 512, HD),
            v(2, 256, HD),
            v(2, 512, HD),
        ],
        24,
        2 * 10**9,
    )
    shapes = [(ROWS, D)] * 2 + [(128, 2 * HD)] * 3
    return pl.pallas_call(
        finish_kernel,
        out_shape=[jax.ShapeDtypeStruct(shape, BF16) for shape in shapes],
    )(pairs, layer_out, grad_residual)


def solution(mesh):
    in_specs = (
        P(("ctx", "exp"), None),
        P("ctx", "exp"),
        P("ctx", "exp"),
        P("ctx", "exp"),
        P("exp", None),
        P(),
        P(("ctx", "exp"), None),
        P(("ctx", "exp"), None),
        P("exp", None, "ctx"),
        P("exp", None, "ctx"),
        P("exp", "ctx", None),
        P(("ctx", "exp"), None),
    )
    out_specs = (
        P(("ctx", "exp"), None),
        P(("ctx", "exp"), None),
        P("ctx", "exp"),
        P("ctx", "exp"),
        P("ctx", "exp"),
    )
    return jax.shard_map(local, mesh=mesh, in_specs=in_specs, out_specs=out_specs, check_vma=False)
```

time: 583 us -> 197 us (0.34)
  waiting for transfers between devices: 448 us -> 0 us
  Pallas kernels: 0 us -> 196 us
  matrix products: 42 us -> 0 us
  blocking collectives: 32 us -> 0 us
  local copies, waits for them, and re-layouts: 23.7 us -> 0 us
  other arithmetic: 17.2 us -> 0 us
  between operations: 14.4 us -> 0.66 us
    reduce_scatter x3 -> x0, waiting for transfers between devices: 251 us -> none  [the longest x1 121 us: local(): lax.psum_scatter(jnp.concatenate((out_term, grad_term), axis=2).astype(jn...]
    pallas_call x0 -> x4, Pallas kernels: none -> 196 us  [the longest x3 195 us: call(): pl.pallas_call(kernel, out_shape=[jax.ShapeDtypeStruct(*shape) for shape...]
    all_gather x3 -> x0, waiting for transfers between devices: 190 us -> none  [the longest x1 81 us: local(): shard_piece = lax.all_gather(arrived, 'ctx', axis=0, tiled=True)]
    dot_general x16 -> x0, matrix products: 42 us -> none  [the longest x1 4.49 us: local(): jnp.einsum('hqk,qhd->khd', softmax_low, grad_heads, preferred_element_typ...]
    all_gather x1 -> x0, blocking collectives: 23.5 us -> none  [local(): lax.all_gather(grad_residual, 'exp', axis=0, tiled=True)]
    concatenate x2 -> x0, other arithmetic: 12.3 us -> none  [the longest x1 7.81 us: local(): jnp.concatenate((out_term, grad_term), axis=2).astype(jnp.bfloat16)]
    reshape x6 -> x0, local copies, waits for them, and re-layouts: 9.54 us -> none  [the longest x1 4.11 us: local(): value_term.reshape(slab_rows * lax.axis_size('ctx'), head_width)]
    all_to_all x1 -> x0, blocking collectives: 8.49 us -> none  [local(): lax.all_to_all(dispatched.reshape(capacity, E, 2 * model_width), 'exp', s...]
  transfers between devices with their start and end apart: 7 -> 0, of which waited for: 7 -> 0; matrix products, arithmetic and copies ran while one was open for 2% -> 0% of each run, Pallas kernels for 0% -> 0%
where the time goes in v1:
time: 197 us
  Pallas kernels  196 us (99%)
    pallas_call x3, Pallas kernels, call(): pl.pallas_call(kernel, out_shape=[jax.ShapeDtypeStruct(*shape) for shape...  195 us

profile of v1, /device:TPU:1, one launch (start us, length us, event | category | flops | bytes accessed | tf_op | source)
XLA Modules:
  0.0 197.1 jit_solution(17585369727501345153)
XLA Ops:
  0.6 60.8 %shard_map.155 = (bf16[256,128]{1,0:T(8,128)(2,1)}, bf16[16,512,128]{2,1,0:T(8,128)(2,1)}, bf16[16,256,256]{2,1,0:T(8,128)(2,1)}, bf16[256,128]{1,0:T(8,128)(2,1...) custom-call(bf16[128,256]{1,0:T(8,128)(2,1)} %q_ref.1, ...), custom_call_target="tpu_custom_call" | custom-call | flops 1000000000 | bytes 16777216 | tf_op jit(solution)/shard_map/pallas_call | solution.py:654
  61.4 94.2 %shard_map.156 = (bf16[16,2048]{1,0:T(8,128)(2,1)}, bf16[16,2048]{1,0:T(8,128)(2,1)}, bf16[128,2048]{1,0:T(8,128)(2,1)}) custom-call(bf16[128,1024]{1,0:T(8,128)(2,1)} %get-tuple-element.17.arrived_ref, bf16[16,2048]{1,0:T(8,128)(2,1)} %get-tuple-element.18.hidden_ref, f32[1,2048]{1,0:T(1,128)} %bitcast.10, s32[2,16]{1,0:T(2,128)} %bitcast.12, ...), custom_call_target="tpu_custom_call" | custom-call | flops 5000000000 | bytes 16777216 | tf_op jit(solution)/shard_map/pallas_call | solution.py:654
  155.6 39.8 %shard_map.157.pairs = bf16[3,2,128,128]{3,2,1,0:T(8,128)(2,1)} custom-call(bf16[128,2048]{1,0:T(8,128)(2,1)} %get-tuple-element.22.slab_ref, bf16[256,2048]{1,0:T(8,128)(2,1)} %ow_ref.3, bf16[256,128]{1,0:T(8,128)(2,1)} %get-tuple-element.23.q_ref, bf16[16,512,128]{2,1,0:T(8,128)(2,1)} %get-tuple-element.24.kv_ref, ...), custom_call_target="tpu_custom_call" | custom-call | flops 2000000000 | bytes 16777216 | tf_op jit(solution)/shard_map/pallas_call | solution.py:654
  195.4 1.7 shard_map.158

commit v2 on v1

v2 whole, which is shorter than its diff:
```python
import math

import jax
import jax.numpy as jnp
from jax import lax
from jax.experimental import pallas as pl
from jax.experimental.pallas import tpu as pltpu
from jax.sharding import PartitionSpec as P

MESH = pl.DeviceIdType.MESH
F32 = jnp.float32
BF16 = jnp.bfloat16
HD = 128
D = 2048
ROWS = 16
CHIPS = 16
N_EXP = 8
CHIP_ROWS = 256
HIDDEN = 200
CHUNK = 1024
EPSILON = 1e-05
MASKED = -1e30
SCALE = 1.0 / math.sqrt(HD)
VMEM_LIMIT = 58 * 1024 * 1024
COPIES = 260

ATTENTION_ORDER = (
    0, 1, 36, 17, 16, 2, 18, 37, 3, 4, 19, 20, 5, 21, 6, 22, 9, 11, 24, 25, 8, 7, 23, 12, 27, 10,
    32, 28, 26, 35, 33, 34,
)
EXPERT_ORDER = (
    0, 33, 1, 32, 16, 17, 49, 34, 4, 48, 50, 2, 35, 36, 3, 18, 19, 20, 5, 6, 38, 37, 7, 51, 9, 22,
    40, 52, 21, 12, 41, 11, 8, 43, 10, 128, 129, 53, 55, 54, 133, 135, 25, 134, 132, 64, 65, 44, 39,
    42, 144, 67, 24, 23, 27, 145, 28, 149, 57, 66, 150, 151, 26, 130, 148, 96, 68, 131, 139, 60, 73,
    97, 56, 59, 58, 136, 137, 98, 138, 80, 146, 147, 81, 69, 153, 71, 100, 155, 152, 154, 113, 112,
    101, 84, 103, 116, 114, 99, 83, 104, 115, 72, 75, 74, 119, 85, 87, 82, 106, 117, 105, 120, 107,
    89, 121, 70, 102, 123, 122, 88, 86, 91, 90, 76, 118, 77, 108, 92, 109, 124, 125, 93,
)
BACKWARD_ORDER = (
    42, 1, 43, 41, 0, 46, 38, 17, 45, 4, 34, 16, 37, 2, 39, 20, 47, 32, 40, 7, 3, 35, 18, 23, 19,
    33, 8, 44, 9, 10, 11, 21, 24, 5, 36, 25, 26, 27, 22, 6, 48, 12, 28, 13, 29,
)
NT = (((1,), (1,)), ((), ()))
TN = (((0,), (0,)), ((), ()))


def rel(dy, dz):
    return dy * 4 + dz


class Net:
    def __init__(self, send, recv):
        self.send, self.recv, self.count, self.started = send, recv, 0, []
        ctx = lax.axis_index("ctx")
        self.exp = lax.axis_index("exp")
        self.core = lax.rem(ctx, 2)
        chip = ctx // 2
        self.y, self.z = chip // 4, lax.rem(chip, 4)
        at = lambda y, z, c: {"ctx": (lax.rem(y, 4) * 4 + lax.rem(z, 4)) * 2 + c}
        self.yp = at(self.y + 1, self.z, self.core)
        self.ym = at(self.y + 3, self.z, self.core)
        self.zp = at(self.y, self.z + 1, self.core)
        self.zm = at(self.y, self.z + 3, self.core)
        self.sibling = at(self.y, self.z, 1 - self.core)
        self.peers = [lax.rem(self.exp + d, N_EXP) for d in range(1, N_EXP)]

    def copy(self, src, dst, device):
        i = self.count
        self.count += 1
        made = pltpu.make_async_remote_copy(
            src_ref=src,
            dst_ref=dst,
            send_sem=self.send.at[i],
            recv_sem=self.recv.at[i],
            device_id=device,
            device_id_type=MESH,
        )
        made.start()
        self.started.append(made)
        return made

    def finish(self):
        for made in self.started:
            made.wait_send()

    def barrier(self, devices):
        sem = pltpu.get_barrier_semaphore()
        for device in devices:
            pl.semaphore_signal(sem, inc=1, device_id=device, device_id_type=MESH)
        pl.semaphore_wait(sem, len(devices))

    def ring_devices(self):
        return [self.yp, self.ym, self.zp, self.zm]

    def peer_devices(self):
        return [{"exp": peer} for peer in self.peers]

    def push(self, src_of, dst):
        return [self.copy(src_of(peer), dst, {"exp": peer}) for peer in self.peers]


def gather_steps(net, full, half, seen=lambda r: None):
    state = {}

    def send_z():
        state["z3"] = net.copy(full(rel(0, 0)), full(rel(0, 3)), net.zp)
        state["z1"] = net.copy(full(rel(0, 0)), full(rel(0, 1)), net.zm)

    def send_y(dz):
        state["y3", dz] = net.copy(full(rel(0, dz)), full(rel(3, dz)), net.yp)
        state["y1", dz] = net.copy(full(rel(0, dz)), full(rel(1, dz)), net.ym)

    def near_z3():
        state["z3"].wait_recv()
        state["h0"] = net.copy(half(rel(0, 3), 0), half(rel(0, 2), 0), net.zp)
        send_y(3)
        seen(rel(0, 3))

    def near_z1():
        state["z1"].wait_recv()
        state["h1"] = net.copy(half(rel(0, 1), 1), half(rel(0, 2), 1), net.zm)
        send_y(1)
        seen(rel(0, 1))

    def far_z():
        state["h0"].wait_recv()
        state["h1"].wait_recv()
        send_y(2)
        seen(rel(0, 2))

    def near_y(dz):
        state["y3", dz].wait_recv()
        state["y1", dz].wait_recv()
        if dz in (0, 2):
            state["g0", dz] = net.copy(half(rel(3, dz), 0), half(rel(2, dz), 0), net.yp)
            state["g1", dz] = net.copy(half(rel(1, dz), 1), half(rel(2, dz), 1), net.ym)
        seen(rel(3, dz))
        seen(rel(1, dz))

    def far_y(dz):
        state["g0", dz].wait_recv()
        state["g1", dz].wait_recv()
        if dz == 0:
            state["f3"] = net.copy(full(rel(2, 0)), full(rel(2, 3)), net.zp)
            state["f1"] = net.copy(full(rel(2, 0)), full(rel(2, 1)), net.zm)
        seen(rel(2, dz))

    def end(dz):
        state["f%d" % dz].wait_recv()
        seen(rel(2, dz))

    return [
        send_z,
        lambda: send_y(0),
        lambda: near_y(0),
        near_z3,
        near_z1,
        lambda: far_y(0),
        far_z,
        lambda: near_y(3),
        lambda: near_y(1),
        lambda: near_y(2),
        lambda: far_y(2),
        lambda: end(3),
        lambda: end(1),
    ]


def reduce_steps(net, full, half, far_y, near_y, far_z, near_z):
    ra, rb, za, zb = far_y.at[0], far_y.at[1], far_z.at[0], far_z.at[1]
    rc, rd = near_y.at[0], near_y.at[1]
    zc, zd, ze, zf = [near_z.at[i] for i in range(4)]
    state = {}

    def add(target, *sources):
        total = target[...].astype(F32)
        for source in sources:
            total = total + source[...].astype(F32)
        target[...] = total.astype(BF16)

    def send_far_z():
        state["e"] = net.copy(full(rel(2, 1)), ze, net.zp)
        state["f"] = net.copy(full(rel(2, 3)), zf, net.zm)

    def send_far_y(dz):
        if dz == 0:
            state["e"].wait_recv()
            state["f"].wait_recv()
            add(full(rel(2, 0)), ze, zf)
        state["a", dz] = net.copy(half(rel(2, dz), 0), ra.at[dz // 2], net.yp)
        state["b", dz] = net.copy(half(rel(2, dz), 1), rb.at[dz // 2], net.ym)

    def send_near(dz):
        if dz in (0, 2):
            state["a", dz].wait_recv()
            state["b", dz].wait_recv()
            add(half(rel(1, dz), 0), ra.at[dz // 2])
            add(half(rel(3, dz), 1), rb.at[dz // 2])
        state["c", dz] = net.copy(full(rel(1, dz)), rc.at[dz], net.yp)
        state["d", dz] = net.copy(full(rel(3, dz)), rd.at[dz], net.ym)

    def collect(dz):
        state["c", dz].wait_recv()
        state["d", dz].wait_recv()
        add(full(rel(0, dz)), rc.at[dz], rd.at[dz])
        if dz == 2:
            state["za"] = net.copy(half(rel(0, 2), 0), za, net.zp)
            state["zb"] = net.copy(half(rel(0, 2), 1), zb, net.zm)

    def send_z1():
        state["za"].wait_recv()
        add(half(rel(0, 1), 0), za)
        state["zc"] = net.copy(full(rel(0, 1)), zc, net.zp)

    def send_z3():
        state["zb"].wait_recv()
        add(half(rel(0, 3), 1), zb)
        state["zd"] = net.copy(full(rel(0, 3)), zd, net.zm)

    def last():
        state["zc"].wait_recv()
        state["zd"].wait_recv()
        add(full(rel(0, 0)), zc, zd)

    return [
        send_far_z,
        lambda: send_far_y(2),
        lambda: send_near(1),
        lambda: send_near(3),
        lambda: send_near(2),
        lambda: send_far_y(0),
        lambda: send_near(0),
        lambda: collect(2),
        lambda: collect(1),
        lambda: collect(3),
        send_z1,
        send_z3,
        lambda: collect(0),
        last,
    ]


def run(order, parts):
    assert sorted(order) == [16 * p + s for p, part in enumerate(parts) for s in range(len(part))]
    for code in order:
        parts[code // 16][code % 16]()


def column(ref, k):
    diagonal = lax.broadcasted_iota(jnp.int32, (ROWS, ROWS), 0) == lax.broadcasted_iota(
        jnp.int32, (ROWS, ROWS), 1
    )
    row = jnp.broadcast_to(ref[k : k + 1, :], (ROWS, ROWS))
    return jnp.sum(jnp.where(diagonal, row, jnp.zeros_like(row)), axis=1, keepdims=True)


def places(ids_ref):
    lanes = lax.broadcasted_iota(jnp.int32, (ROWS, 128), 1)
    ids = [column(ids_ref, k) for k in range(2)]
    chosen = [(lanes == one).astype(F32) for one in ids]
    lower = (
        lax.broadcasted_iota(jnp.int32, (ROWS, ROWS), 1)
        < lax.broadcasted_iota(jnp.int32, (ROWS, ROWS), 0)
    ).astype(BF16)
    earlier = jnp.dot(lower, (chosen[0] + chosen[1]).astype(BF16), preferred_element_type=F32)
    found = []
    for one, hot in zip(ids, chosen):
        rank = jnp.sum(earlier * hot, axis=1, keepdims=True).astype(jnp.int32)
        place = (one >> 1) * 16 + (one & 1) * 2 + rank
        found.append(jnp.where(rank < 2, place, -1000))
    return found


def one_hot(place, quarter):
    lanes = lax.broadcasted_iota(jnp.int32, (ROWS, 128), 1)
    return (lanes == place + 4 * quarter).astype(BF16)


def packing(quarter, transposed):
    shape, slot_dim = ((128, 32), 1) if transposed else ((32, 128), 0)
    slot = lax.broadcasted_iota(jnp.int32, shape, slot_dim)
    packed = lax.broadcasted_iota(jnp.int32, shape, 1 - slot_dim)
    want = ((slot & 15) >> 1) * 16 + quarter * 4 + (slot >> 4) * 2 + (slot & 1)
    return (packed == want).astype(BF16)


def layer_kernel(
    q_ref,
    k_ref,
    v_ref,
    residual_ref,
    gain_ref,
    ids_ref,
    gw_ref,
    go_ref,
    ow_hbm,
    wg_hbm,
    wu_hbm,
    wd_hbm,
    layer_out,
    residual_out,
    pairs,
    ow_ref,
    queries,
    kv,
    softmax,
    attended_rows,
    scores,
    row_top,
    row_sum,
    att_pair,
    partial,
    pieces,
    packed,
    arrived,
    slots,
    sums,
    gates,
    ups,
    downs,
    gate_part,
    up_part,
    actives,
    grad_gates,
    grad_ups,
    far_y,
    near_y,
    far_z,
    near_z,
    packed_back,
    returned,
    slab,
    grads,
    grad_heads,
    grad_sums,
    dq_rows,
    dq_other,
    att_far_y,
    att_near_y,
    att_far_z,
    att_near_z,
    load_sem,
    send,
    recv,
):
    net = Net(send, recv)
    core, me = net.core, net.exp
    own_rows = pl.ds(pl.multiple_of(core * 128, 128), 128)
    other_rows = pl.ds(pl.multiple_of((1 - core) * 128, 128), 128)
    own_values = pl.ds(pl.multiple_of(256 + core * 128, 128), 128)
    other_values = pl.ds(pl.multiple_of(256 + (1 - core) * 128, 128), 128)

    def piece(ref, peer):
        return ref.at[pl.ds(pl.multiple_of(peer * ROWS, ROWS), ROWS), :]

    def mine(ref):
        return jnp.where(core == 0, ref[:, :128], ref[:, 128:])

    weights = ((wg_hbm, gates), (wu_hbm, ups), (wd_hbm, downs))
    loads = [pltpu.make_async_copy(ow_hbm, ow_ref, load_sem.at[0])]
    for i, (source, target) in enumerate(weights):
        loads.append(pltpu.make_async_copy(source, target.at[0], load_sem.at[i + 1]))
    for made in loads:
        made.start()
    net.barrier(net.ring_devices() + [net.sibling] + net.peer_devices())

    exchange = [
        net.copy(k_ref.at[:, other_rows], kv.at[0, own_rows, :], net.sibling),
        net.copy(q_ref.at[:, other_rows], queries.at[own_rows, :], net.sibling),
        net.copy(v_ref.at[:, other_rows], kv.at[0, own_values, :], net.sibling),
    ]
    kv[0, own_rows, :] = mine(k_ref)
    kv[0, own_values, :] = mine(v_ref)
    queries[own_rows, :] = mine(q_ref)

    chip = net.y * 4 + net.z

    def score_block(r):
        dy, dz = r // 4, r % 4
        other = lax.rem(net.y + dy, 4) * 4 + lax.rem(net.z + dz, 4)
        s = lax.dot_general(queries[...], kv[r, :256, :], NT, preferred_element_type=F32) * SCALE
        row = lax.broadcasted_iota(jnp.int32, (CHIP_ROWS, CHIP_ROWS), 0) + chip * CHIP_ROWS
        place = lax.broadcasted_iota(jnp.int32, (CHIP_ROWS, CHIP_ROWS), 1) + other * CHIP_ROWS
        s = jnp.where(place <= row, s, MASKED)
        scores[r] = s
        row_top[...] = jnp.maximum(row_top[...], jnp.maximum(s[:, :128], s[:, 128:]))

    row_top[...] = jnp.full((CHIP_ROWS, 128), MASKED, F32)
    row_sum[...] = jnp.zeros((CHIP_ROWS, 128), F32)

    def raise_blocks(quarter):
        m = jnp.max(row_top[...], axis=1, keepdims=True)

        def one(r, total):
            e = jnp.exp(scores[r] - m)
            scores[r] = e
            return total + (e[:, :128] + e[:, 128:])

        row_sum[...] = lax.fori_loop(4 * quarter, 4 * quarter + 4, one, row_sum[...])

    def pair(ref, start, seen):
        full = lambda r: ref.at[r, pl.ds(start, 256), :]
        half = lambda r, h: ref.at[r, pl.ds(start + h * 128, 128), :]
        return gather_steps(net, full, half, seen)

    raises = [lambda i=i: raise_blocks(i) for i in range(4)]
    for made in exchange:
        made.wait_recv()
    other_weights = []

    def send_weights():
        for source, target in weights:
            other_weights.append(net.copy(source, target.at[1], net.sibling))

    attention = [
        pair(kv, 0, score_block),
        pair(kv, 256, lambda r: None),
        raises + [lambda: score_block(0), send_weights],
    ]
    run(ATTENTION_ORDER, attention)
    inverse = 1.0 / jnp.sum(row_sum[...], axis=1, keepdims=True)

    def attend(r, acc):
        low = (scores[r] * inverse).astype(BF16)
        softmax[r] = low
        return acc + jnp.dot(low, kv[r, 256:, :], preferred_element_type=F32)

    attended = lax.fori_loop(0, CHIPS, attend, jnp.zeros((CHIP_ROWS, HD), F32))
    attended_rows[...] = attended.astype(BF16)
    swap = net.copy(attended_rows.at[other_rows, :], att_pair.at[core], net.sibling)
    att_pair[core] = attended_rows[own_rows, :]
    for made in loads:
        made.wait()
    swap.wait_recv()

    for n in range(4):
        columns = pl.ds(n * 512, 512)
        partial[:, columns] = (
            jnp.dot(att_pair[0], ow_ref[:128, columns], preferred_element_type=F32)
            + jnp.dot(att_pair[1], ow_ref[128:, columns], preferred_element_type=F32)
        ).astype(BF16)
    moved = net.push(lambda peer: piece(partial, peer), piece(pieces, me))
    piece(pieces, me)[...] = piece(partial, me)[...]
    found = places(ids_ref)
    weight = [column(gw_ref, k) for k in range(2)]
    grad_out = go_ref[...].astype(F32)
    weighted = [(weight[k] * grad_out).astype(BF16) for k in range(2)]
    for made in moved:
        made.wait_recv()
    projected = pieces[0:ROWS, :].astype(F32)
    for j in range(1, N_EXP):
        projected = projected + pieces[j * ROWS : (j + 1) * ROWS, :].astype(F32)
    wide = (residual_ref[...].astype(F32) + projected).astype(BF16).astype(F32)
    inverse_norm = lax.rsqrt(jnp.mean(wide * wide, axis=1, keepdims=True) + EPSILON)
    normed = (wide * inverse_norm * gain_ref[...]).astype(BF16)
    spread = jnp.zeros((128, CHUNK), F32)
    for quarter in range(4):
        for k in range(2):
            source = normed if quarter < 2 else weighted[k]
            low = (quarter % 2) * CHUNK
            spread = spread + lax.dot_general(
                one_hot(found[k], quarter),
                source[:, low : low + CHUNK],
                TN,
                preferred_element_type=F32,
            )
    packed[...] = spread.astype(BF16)
    moved = net.push(lambda peer: piece(packed, peer), piece(arrived, me))
    piece(arrived, me)[...] = piece(packed, me)[...]
    for made in moved:
        made.wait_recv()
    for quarter in range(4):
        rows = jnp.dot(packing(quarter, False), arrived[...], preferred_element_type=F32)
        rows = rows.astype(BF16)
        for e in range(2):
            slots[e, 0:ROWS, quarter * CHUNK : (quarter + 1) * CHUNK] = rows[e * 16 : e * 16 + 16]

    def block(ref, e, part):
        full = lambda r: ref.at[e, pl.ds(r * ROWS, ROWS), pl.ds(part * D, D)]
        half = lambda r, h: ref.at[
            e, pl.ds(r * ROWS, ROWS), pl.ds(part * D + h * CHUNK, CHUNK)
        ]
        return full, half

    parts = [(e, part) for e in range(2) for part in range(2)]
    experts = [gather_steps(net, *block(slots, e, part)) for e, part in parts]
    for i, (e, part) in enumerate(parts):
        buffers = [ref.at[i] for ref in (far_y, near_y, far_z, near_z)]
        experts.append(reduce_steps(net, *block(sums, e, part), *buffers))

    def compute_steps(e):
        def enter(half):
            inputs = slots[e, :, :D]
            gate = lax.dot_general(inputs, gates[half, e], NT, preferred_element_type=F32)
            up = lax.dot_general(inputs, ups[half, e], NT, preferred_element_type=F32)
            gate_part[e, half] = gate
            up_part[e, half] = up
            actives[e, half] = (gate * jax.nn.sigmoid(gate) * up).astype(BF16)

        def enter_grad(half):
            grad = lax.dot_general(
                slots[e, :, D:], downs[half, e], NT, preferred_element_type=F32
            )
            gate, up = gate_part[e, half], up_part[e, half]
            s = jax.nn.sigmoid(gate)
            grad_gates[e, half] = (grad * up * s * (1.0 + gate * (1.0 - s))).astype(BF16)
            grad_ups[e, half] = (grad * gate * s).astype(BF16)

        def leave(n, start, terms):
            columns = pl.ds(n * 512, 512)
            total = jnp.zeros((CHIP_ROWS, 512), F32)
            for half in range(2):
                for rows, matrix in terms:
                    total = total + jnp.dot(
                        rows[e, half], matrix[half, e, :, columns], preferred_element_type=F32
                    )
            sums[e, :, pl.ds(start + n * 512, 512)] = total.astype(BF16)

        out_terms = [(actives, downs)]
        grad_terms = [(grad_gates, gates), (grad_ups, ups)]
        steps = [lambda half=half: enter(half) for half in range(2)]
        steps += [lambda half=half: enter_grad(half) for half in range(2)]
        steps += [lambda n=n: leave(n, 0, out_terms) for n in range(4)]
        steps += [lambda n=n: leave(n, D, grad_terms) for n in range(4)]
        return steps

    experts += [compute_steps(e) for e in range(2)]
    for made in other_weights:
        made.wait_recv()
    run(EXPERT_ORDER, experts)

    spread = jnp.zeros((128, CHUNK), F32)
    for quarter in range(4):
        columns = slice(quarter * CHUNK, (quarter + 1) * CHUNK)
        both = jnp.concatenate((sums[0, 0:ROWS, columns], sums[1, 0:ROWS, columns]), axis=0)
        spread = spread + jnp.dot(packing(quarter, True), both, preferred_element_type=F32)
    packed_back[...] = spread.astype(BF16)
    moved = net.push(lambda peer: piece(packed_back, peer), piece(returned, me))
    piece(returned, me)[...] = piece(packed_back, me)[...]
    for made in moved:
        made.wait_recv()

    def pick(k, quarter):
        return jnp.dot(one_hot(found[k], quarter), returned[...], preferred_element_type=F32)

    grad_normed = jnp.concatenate([pick(0, q) + pick(1, q) for q in (2, 3)], axis=1)
    scaled = gain_ref[...] * grad_normed
    cube = inverse_norm * inverse_norm * inverse_norm
    grad_hidden = grad_out + (
        inverse_norm * scaled - wide * cube * jnp.mean(wide * scaled, axis=1, keepdims=True)
    )
    residual_out[...] = grad_hidden.astype(BF16)
    moved = net.push(lambda peer: residual_out, piece(slab, me))
    piece(slab, me)[...] = residual_out[...]
    for quarter in range(2):
        columns = slice(quarter * CHUNK, (quarter + 1) * CHUNK)
        mixture = weight[0] * pick(0, quarter) + weight[1] * pick(1, quarter)
        layer_out[:, columns] = (wide[:, columns] + mixture).astype(BF16)
    for made in moved:
        made.wait_recv()

    for head in range(2):
        grads[head] = lax.dot_general(
            slab[...], ow_ref[head * 128 : head * 128 + 128, :], NT, preferred_element_type=F32
        ).astype(BF16)
    swap = net.copy(grads.at[1 - core], grad_heads.at[own_rows, :], net.sibling)
    grad_heads[own_rows, :] = grads[core]
    swap.wait_recv()
    grad_head = grad_heads[...]
    delta = jnp.sum(
        grad_head.astype(F32) * attended_rows[...].astype(F32), axis=1, keepdims=True
    )
    dq_rows[...] = jnp.zeros((CHIP_ROWS, HD), F32)

    def back(r):
        low = softmax[r]
        grad_prob = lax.dot_general(grad_head, kv[r, 256:, :], NT, preferred_element_type=F32)
        grad_score = (low.astype(F32) * (grad_prob - delta)).astype(BF16)
        dq_rows[...] += jnp.dot(grad_score, kv[r, :256, :], preferred_element_type=F32)
        grad_sums[r, :256, :] = (
            lax.dot_general(grad_score, queries[...], TN, preferred_element_type=F32) * SCALE
        ).astype(BF16)
        grad_sums[r, 256:, :] = lax.dot_general(
            low, grad_head, TN, preferred_element_type=F32
        ).astype(BF16)

    swaps = []

    def send_queries():
        dq_other[...] = (dq_rows[other_rows, :] * SCALE).astype(BF16)
        swaps.append(net.copy(dq_other, pairs.at[0, core], net.sibling))
        pairs[0, core] = (dq_rows[own_rows, :] * SCALE).astype(BF16)

    def key_sums(i):
        full = lambda r: grad_sums.at[r, pl.ds(i * 256, 256), :]
        half = lambda r, h: grad_sums.at[r, pl.ds(i * 256 + h * 128, 128), :]
        return reduce_steps(
            net,
            full,
            half,
            att_far_y.at[i],
            att_near_y.at[i],
            att_far_z.at[i],
            att_near_z.at[i],
        )

    backs = [lambda r=r: back(r) for r in range(CHIPS)]
    run(BACKWARD_ORDER, [key_sums(0), key_sums(1), backs, [send_queries]])
    swaps.append(net.copy(grad_sums.at[0, other_rows, :], pairs.at[1, core], net.sibling))
    swaps.append(net.copy(grad_sums.at[0, other_values, :], pairs.at[2, core], net.sibling))
    pairs[1, core] = grad_sums[0, own_rows, :]
    pairs[2, core] = grad_sums[0, own_values, :]
    for made in swaps:
        made.wait_recv()
    net.finish()


def finish_kernel(pairs, layer_ref, residual_ref, layer_out, residual_out, *outs):
    layer_out[...] = layer_ref[...]
    residual_out[...] = residual_ref[...]
    for i, out in enumerate(outs):
        out[:, :128] = pairs[i, 0]
        out[:, 128:] = pairs[i, 1]


def local(
    residual,
    query_states,
    key_states,
    value_states,
    out_weight,
    norm_gain,
    expert_ids,
    gate_weights,
    gate_matrix,
    up_matrix,
    down_matrix,
    grad_out,
):
    inputs = (
        query_states,
        key_states,
        value_states,
        residual,
        norm_gain.reshape(1, D),
        expert_ids.T,
        gate_weights.T,
        grad_out,
        out_weight,
        gate_matrix.transpose(0, 2, 1),
        up_matrix.transpose(0, 2, 1),
        down_matrix,
    )
    v = lambda *shape: pltpu.VMEM(shape, BF16)
    vmem = pl.BlockSpec(memory_space=pltpu.VMEM)
    results = [(ROWS, D), (ROWS, D), (3, 2, 128, HD)]
    layer_out, grad_residual, pairs = pl.pallas_call(
        layer_kernel,
        out_shape=[jax.ShapeDtypeStruct(shape, BF16) for shape in results],
        in_specs=[vmem] * 8 + [pl.BlockSpec(memory_space=pl.ANY)] * 4,
        out_specs=[vmem] * 3,
        scratch_shapes=[
            v(256, D),
            v(CHIP_ROWS, HD),
            v(CHIPS, 512, HD),
            v(CHIPS, CHIP_ROWS, CHIP_ROWS),
            v(CHIP_ROWS, HD),
            pltpu.VMEM((CHIPS, CHIP_ROWS, CHIP_ROWS), F32),
            pltpu.VMEM((CHIP_ROWS, 128), F32),
            pltpu.VMEM((CHIP_ROWS, 128), F32),
            v(2, 128, HD),
            v(128, D),
            v(128, D),
            v(128, CHUNK),
            v(128, CHUNK),
            v(2, CHIP_ROWS, 2 * D),
            v(2, CHIP_ROWS, 2 * D),
            v(2, 2, HIDDEN, D),
            v(2, 2, HIDDEN, D),
            v(2, 2, HIDDEN, D),
            pltpu.VMEM((2, 2, CHIP_ROWS, HIDDEN), F32),
            pltpu.VMEM((2, 2, CHIP_ROWS, HIDDEN), F32),
            v(2, 2, CHIP_ROWS, HIDDEN),
            v(2, 2, CHIP_ROWS, HIDDEN),
            v(2, 2, CHIP_ROWS, HIDDEN),
            v(4, 2, 2, ROWS, CHUNK),
            v(4, 2, 4, ROWS, D),
            v(4, 2, ROWS, CHUNK),
            v(4, 4, ROWS, D),
            v(128, CHUNK),
            v(128, CHUNK),
            v(128, D),
            v(2, 128, HD),
            v(CHIP_ROWS, HD),
            v(CHIPS, 512, HD),
            pltpu.VMEM((CHIP_ROWS, HD), F32),
            v(128, HD),
            v(2, 2, 2, 128, HD),
            v(2, 2, 4, 256, HD),
            v(2, 2, 128, HD),
            v(2, 4, 256, HD),
            pltpu.SemaphoreType.DMA((4,)),
            pltpu.SemaphoreType.DMA((COPIES,)),
            pltpu.SemaphoreType.DMA((COPIES,)),
        ],
        compiler_params=pltpu.CompilerParams(
            collective_id=0, has_side_effects=True, vmem_limit_bytes=VMEM_LIMIT
        ),
        cost_estimate=pl.CostEstimate(
            flops=8 * 10**9, bytes_accessed=1 << 24, transcendentals=1 << 21
        ),
    )(*inputs)
    shapes = [(ROWS, D)] * 2 + [(128, 2 * HD)] * 3
    return pl.pallas_call(
        finish_kernel,
        out_shape=[jax.ShapeDtypeStruct(shape, BF16) for shape in shapes],
    )(pairs, layer_out, grad_residual)


def solution(mesh):
    in_specs = (
        P(("ctx", "exp"), None),
        P("ctx", "exp"),
        P("ctx", "exp"),
        P("ctx", "exp"),
        P("exp", None),
        P(),
        P(("ctx", "exp"), None),
        P(("ctx", "exp"), None),
        P("exp", None, "ctx"),
        P("exp", None, "ctx"),
        P("exp", "ctx", None),
        P(("ctx", "exp"), None),
    )
    out_specs = (
        P(("ctx", "exp"), None),
        P(("ctx", "exp"), None),
        P("ctx", "exp"),
        P("ctx", "exp"),
        P("ctx", "exp"),
    )
    return jax.shard_map(local, mesh=mesh, in_specs=in_specs, out_specs=out_specs, check_vma=False)
```

time: 197 us -> 164 us (0.83)
  Pallas kernels: 196 us -> 163 us
    pallas_call x3 -> x1, Pallas kernels: 195 us -> 161 us  [local(): pl.pallas_call(layer_kernel, out_shape=[jax.ShapeDtypeStruct(shape, BF16)...]
where the time goes in v2:
time: 164 us; the launch traced here: 163 us
  Pallas kernels  163 us (99%)
    pallas_call x1, Pallas kernels, local(): pl.pallas_call(layer_kernel, out_shape=[jax.ShapeDtypeStruct(shape, BF16)...  161 us

profile of v2, /device:TPU:1, one launch (start us, length us, event | category | flops | bytes accessed | tf_op | source)
XLA Modules:
  0.0 163.4 jit_solution(2615755854833423356)
XLA Ops:
  0.6 161.1 %shard_map.155 = (bf16[16,2048]{1,0:T(8,128)(2,1)}, bf16[16,2048]{1,0:T(8,128)(2,1)}, bf16[3,2,128,128]{3,2,1,0:T(8,128)(2,1)}) custom-call(bf16[128,256]{1,0:T(8,128)(2,1)} %q_ref.1, bf16[128,256]{1,0:T(8,128)(2,1)} %k_ref.1, bf16[128,256]{1,0:T(8,128)(2,1)} %v_ref.1, bf16[16,2048]{1,0:T(8,128)(2,1)} %residual_ref.1, f32[1,2048]{1,0:T(1,128)} %bitcast.7, ...), custom_call_target="tpu_custom_call" | custom-call | flops 8000000000 | bytes 16777216 | tf_op jit(solution)/shard_map/pallas_call | solution.py:657
  161.7 1.7 %shard_map.156 = (bf16[16,2048]{1,0:T(8,128)(2,1)}, bf16[16,2048]{1,0:T(8,128)(2,1)}, bf16[128,256]{1,0:T(8,128)(2,1)}, bf16[128,256]{1,0:T(8,128)(2,1)}, bf16[128,256]{1,0:T(8,128)(2,1)}) custom-call(bf16[3,2,128,128]{3,2,1,0:T(8,128)(2,1)} %get-tuple-element.8.pairs, bf16[16,2048]{1,0:T(8,128)(2,1)} %get-tuple-element.9.layer_ref, ...), custom_call_target="tpu_custom_call" | custom-call | tf_op jit(solution)/shard_map/pallas_call | solution.py:714

commit v3 on v2

--- a/solution.py
+++ b/solution.py
@@ -18,27 +18,25 @@
 CHIP_ROWS = 256
 HIDDEN = 200
 CHUNK = 1024
+QUARTER = 512
 EPSILON = 1e-05
 MASKED = -1e30
 SCALE = 1.0 / math.sqrt(HD)
 VMEM_LIMIT = 58 * 1024 * 1024
-COPIES = 260
-
-ATTENTION_ORDER = (
-    0, 1, 36, 17, 16, 2, 18, 37, 3, 4, 19, 20, 5, 21, 6, 22, 9, 11, 24, 25, 8, 7, 23, 12, 27, 10,
-    32, 28, 26, 35, 33, 34,
-)
-EXPERT_ORDER = (
-    0, 33, 1, 32, 16, 17, 49, 34, 4, 48, 50, 2, 35, 36, 3, 18, 19, 20, 5, 6, 38, 37, 7, 51, 9, 22,
-    40, 52, 21, 12, 41, 11, 8, 43, 10, 128, 129, 53, 55, 54, 133, 135, 25, 134, 132, 64, 65, 44, 39,
-    42, 144, 67, 24, 23, 27, 145, 28, 149, 57, 66, 150, 151, 26, 130, 148, 96, 68, 131, 139, 60, 73,
-    97, 56, 59, 58, 136, 137, 98, 138, 80, 146, 147, 81, 69, 153, 71, 100, 155, 152, 154, 113, 112,
-    101, 84, 103, 116, 114, 99, 83, 104, 115, 72, 75, 74, 119, 85, 87, 82, 106, 117, 105, 120, 107,
-    89, 121, 70, 102, 123, 122, 88, 86, 91, 90, 76, 118, 77, 108, 92, 109, 124, 125, 93,
-)
-BACKWARD_ORDER = (
-    42, 1, 43, 41, 0, 46, 38, 17, 45, 4, 34, 16, 37, 2, 39, 20, 47, 32, 40, 7, 3, 35, 18, 23, 19,
-    33, 8, 44, 9, 10, 11, 21, 24, 5, 36, 25, 26, 27, 22, 6, 48, 12, 28, 13, 29,
+COPIES = 270
+
+ORDER = (
+    0, 1, 16, 258, 17, 2, 257, 18, 3, 4, 20, 19, 5, 21, 259, 80, 6, 256, 8, 7, 22, 24, 48, 264, 9,
+    12, 23, 25, 81, 11, 10, 240, 243, 242, 27, 241, 26, 28, 260, 49, 52, 261, 83, 82, 51, 84, 262,
+    55, 54, 86, 85, 263, 32, 33, 64, 87, 65, 57, 50, 34, 66, 35, 36, 56, 37, 68, 38, 67, 89, 53, 69,
+    40, 58, 91, 41, 39, 70, 43, 44, 42, 97, 96, 59, 60, 99, 73, 98, 105, 106, 92, 88, 90, 104, 107,
+    145, 144, 146, 75, 76, 72, 71, 74, 113, 112, 114, 115, 121, 148, 120, 122, 123, 176, 177, 100,
+    147, 102, 103, 119, 101, 118, 151, 129, 180, 179, 178, 128, 116, 149, 181, 183, 132, 153, 155,
+    152, 154, 185, 182, 184, 186, 187, 150, 135, 130, 117, 161, 156, 157, 131, 188, 189, 265, 160,
+    164, 167, 266, 137, 139, 162, 133, 163, 136, 138, 168, 165, 169, 171, 134, 166, 170, 267, 268,
+    202, 225, 203, 201, 224, 208, 209, 207, 200, 206, 198, 228, 194, 204, 199, 212, 227, 231, 205,
+    197, 226, 215, 211, 172, 140, 141, 173, 210, 269, 196, 213, 195, 233, 229, 193, 232, 234, 235,
+    216, 218, 217, 219, 214, 192, 271, 270, 230, 220, 236, 237, 221,
 )
 NT = (((1,), (1,)), ((), ()))
 TN = (((0,), (0,)), ((), ()))
@@ -327,8 +325,9 @@
     near_y,
     far_z,
     near_z,
-    packed_back,
     returned,
+    hidden_rows,
+    delta_rows,
     slab,
     grads,
     grad_heads,
@@ -398,82 +397,107 @@
 
         row_sum[...] = lax.fori_loop(4 * quarter, 4 * quarter + 4, one, row_sum[...])
 
-    def pair(ref, start, seen):
-        full = lambda r: ref.at[r, pl.ds(start, 256), :]
-        half = lambda r, h: ref.at[r, pl.ds(start + h * 128, 128), :]
+    def pair(start, seen):
+        full = lambda r: kv.at[r, pl.ds(start, 256), :]
+        half = lambda r, h: kv.at[r, pl.ds(start + h * 128, 128), :]
         return gather_steps(net, full, half, seen)
 
-    raises = [lambda i=i: raise_blocks(i) for i in range(4)]
-    for made in exchange:
-        made.wait_recv()
-    other_weights = []
+    keep = {}
 
     def send_weights():
-        for source, target in weights:
-            other_weights.append(net.copy(source, target.at[1], net.sibling))
-
-    attention = [
-        pair(kv, 0, score_block),
-        pair(kv, 256, lambda r: None),
-        raises + [lambda: score_block(0), send_weights],
-    ]
-    run(ATTENTION_ORDER, attention)
-    inverse = 1.0 / jnp.sum(row_sum[...], axis=1, keepdims=True)
-
-    def attend(r, acc):
-        low = (scores[r] * inverse).astype(BF16)
-        softmax[r] = low
-        return acc + jnp.dot(low, kv[r, 256:, :], preferred_element_type=F32)
-
-    attended = lax.fori_loop(0, CHIPS, attend, jnp.zeros((CHIP_ROWS, HD), F32))
-    attended_rows[...] = attended.astype(BF16)
-    swap = net.copy(attended_rows.at[other_rows, :], att_pair.at[core], net.sibling)
-    att_pair[core] = attended_rows[own_rows, :]
-    for made in loads:
-        made.wait()
-    swap.wait_recv()
-
-    for n in range(4):
-        columns = pl.ds(n * 512, 512)
-        partial[:, columns] = (
-            jnp.dot(att_pair[0], ow_ref[:128, columns], preferred_element_type=F32)
-            + jnp.dot(att_pair[1], ow_ref[128:, columns], preferred_element_type=F32)
-        ).astype(BF16)
-    moved = net.push(lambda peer: piece(partial, peer), piece(pieces, me))
-    piece(pieces, me)[...] = piece(partial, me)[...]
+        keep["weights"] = [net.copy(hbm, at.at[1], net.sibling) for hbm, at in weights]
+
+    def wait_for(name):
+        for made in keep.pop(name):
+            made.wait_recv()
+
     found = places(ids_ref)
     weight = [column(gw_ref, k) for k in range(2)]
-    grad_out = go_ref[...].astype(F32)
-    weighted = [(weight[k] * grad_out).astype(BF16) for k in range(2)]
-    for made in moved:
-        made.wait_recv()
-    projected = pieces[0:ROWS, :].astype(F32)
-    for j in range(1, N_EXP):
-        projected = projected + pieces[j * ROWS : (j + 1) * ROWS, :].astype(F32)
-    wide = (residual_ref[...].astype(F32) + projected).astype(BF16).astype(F32)
-    inverse_norm = lax.rsqrt(jnp.mean(wide * wide, axis=1, keepdims=True) + EPSILON)
-    normed = (wide * inverse_norm * gain_ref[...]).astype(BF16)
-    spread = jnp.zeros((128, CHUNK), F32)
-    for quarter in range(4):
-        for k in range(2):
-            source = normed if quarter < 2 else weighted[k]
-            low = (quarter % 2) * CHUNK
-            spread = spread + lax.dot_general(
-                one_hot(found[k], quarter),
-                source[:, low : low + CHUNK],
-                TN,
-                preferred_element_type=F32,
+
+    def exchange_slots(name, source, target):
+        keep[name] = net.push(lambda peer: piece(source, peer), piece(target, me))
+        piece(target, me)[...] = piece(source, me)[...]
+
+    def pack(part, rows_of):
+        for quarter in range(4):
+            columns = slice(quarter * QUARTER, (quarter + 1) * QUARTER)
+            spread = rows_of(quarter, columns)
+            total = spread if quarter == 0 else total + spread
+        packed[part] = total.astype(BF16)
+
+    def dispatch_weighted():
+        grad_out = go_ref[...].astype(F32)
+        weighted = [(weight[k] * grad_out).astype(BF16) for k in range(2)]
+
+        def rows_of(quarter, columns):
+            return sum(
+                lax.dot_general(
+                    one_hot(found[k], quarter),
+                    weighted[k][:, columns],
+                    TN,
+                    preferred_element_type=F32,
+                )
+                for k in range(2)
             )
-    packed[...] = spread.astype(BF16)
-    moved = net.push(lambda peer: piece(packed, peer), piece(arrived, me))
-    piece(arrived, me)[...] = piece(packed, me)[...]
-    for made in moved:
-        made.wait_recv()
-    for quarter in range(4):
-        rows = jnp.dot(packing(quarter, False), arrived[...], preferred_element_type=F32)
-        rows = rows.astype(BF16)
-        for e in range(2):
-            slots[e, 0:ROWS, quarter * CHUNK : (quarter + 1) * CHUNK] = rows[e * 16 : e * 16 + 16]
+
+        pack(1, rows_of)
+        exchange_slots("arrived1", packed.at[1], arrived.at[1])
+
+    def unpack(part):
+        wait_for("arrived%d" % part)
+        for quarter in range(4):
+            rows = jnp.dot(packing(quarter, False), arrived[part], preferred_element_type=F32)
+            rows = rows.astype(BF16)
+            low = part * D + quarter * QUARTER
+            for e in range(2):
+                slots[e, 0:ROWS, low : low + QUARTER] = rows[e * ROWS : (e + 1) * ROWS]
+
+    def attend():
+        inverse = 1.0 / jnp.sum(row_sum[...], axis=1, keepdims=True)
+
+        def one(r, acc):
+            low = (scores[r] * inverse).astype(BF16)
+            softmax[r] = low
+            return acc + jnp.dot(low, kv[r, 256:, :], preferred_element_type=F32)
+
+        attended = lax.fori_loop(0, CHIPS, one, jnp.zeros((CHIP_ROWS, HD), F32))
+        attended_rows[...] = attended.astype(BF16)
+        keep["attended"] = [
+            net.copy(attended_rows.at[other_rows, :], att_pair.at[core], net.sibling)
+        ]
+        att_pair[core] = attended_rows[own_rows, :]
+
+    def project():
+        for made in loads:
+            made.wait()
+        wait_for("attended")
+        for n in range(4):
+            columns = pl.ds(n * 512, 512)
+            partial[:, columns] = (
+                jnp.dot(att_pair[0], ow_ref[:128, columns], preferred_element_type=F32)
+                + jnp.dot(att_pair[1], ow_ref[128:, columns], preferred_element_type=F32)
+            ).astype(BF16)
+        exchange_slots("projected", partial, pieces)
+
+    def inverse_norm():
+        wide = hidden_rows[...]
+        return lax.rsqrt(jnp.mean(wide * wide, axis=1, keepdims=True) + EPSILON)
+
+    def norm():
+        wait_for("projected")
+        projected = pieces[0:ROWS, :].astype(F32)
+        for j in range(1, N_EXP):
+            projected = projected + pieces[j * ROWS : (j + 1) * ROWS, :].astype(F32)
+        hidden = (residual_ref[...].astype(F32) + projected).astype(BF16)
+        hidden_rows[...] = hidden.astype(F32)
+        normed = (hidden_rows[...] * inverse_norm() * gain_ref[...]).astype(BF16)
+
+        def rows_of(quarter, columns):
+            hot = one_hot(found[0], quarter) + one_hot(found[1], quarter)
+            return lax.dot_general(hot, normed[:, columns], TN, preferred_element_type=F32)
+
+        pack(0, rows_of)
+        exchange_slots("arrived0", packed.at[0], arrived.at[0])
 
     def block(ref, e, part):
         full = lambda r: ref.at[e, pl.ds(r * ROWS, ROWS), pl.ds(part * D, D)]
@@ -483,10 +507,11 @@
         return full, half
 
     parts = [(e, part) for e in range(2) for part in range(2)]
-    experts = [gather_steps(net, *block(slots, e, part)) for e, part in parts]
+    gathers = [gather_steps(net, *block(slots, e, part)) for e, part in parts]
+    reduces = []
     for i, (e, part) in enumerate(parts):
         buffers = [ref.at[i] for ref in (far_y, near_y, far_z, near_z)]
-        experts.append(reduce_steps(net, *block(sums, e, part), *buffers))
+        reduces.append(reduce_steps(net, *block(sums, e, part), *buffers))
 
     def compute_steps(e):
         def enter(half):
@@ -524,58 +549,66 @@
         steps += [lambda n=n: leave(n, D, grad_terms) for n in range(4)]
         return steps
 
-    experts += [compute_steps(e) for e in range(2)]
-    for made in other_weights:
-        made.wait_recv()
-    run(EXPERT_ORDER, experts)
-
-    spread = jnp.zeros((128, CHUNK), F32)
-    for quarter in range(4):
-        columns = slice(quarter * CHUNK, (quarter + 1) * CHUNK)
-        both = jnp.concatenate((sums[0, 0:ROWS, columns], sums[1, 0:ROWS, columns]), axis=0)
-        spread = spread + jnp.dot(packing(quarter, True), both, preferred_element_type=F32)
-    packed_back[...] = spread.astype(BF16)
-    moved = net.push(lambda peer: piece(packed_back, peer), piece(returned, me))
-    piece(returned, me)[...] = piece(packed_back, me)[...]
-    for made in moved:
-        made.wait_recv()
-
-    def pick(k, quarter):
-        return jnp.dot(one_hot(found[k], quarter), returned[...], preferred_element_type=F32)
-
-    grad_normed = jnp.concatenate([pick(0, q) + pick(1, q) for q in (2, 3)], axis=1)
-    scaled = gain_ref[...] * grad_normed
-    cube = inverse_norm * inverse_norm * inverse_norm
-    grad_hidden = grad_out + (
-        inverse_norm * scaled - wide * cube * jnp.mean(wide * scaled, axis=1, keepdims=True)
-    )
-    residual_out[...] = grad_hidden.astype(BF16)
-    moved = net.push(lambda peer: residual_out, piece(slab, me))
-    piece(slab, me)[...] = residual_out[...]
-    for quarter in range(2):
-        columns = slice(quarter * CHUNK, (quarter + 1) * CHUNK)
-        mixture = weight[0] * pick(0, quarter) + weight[1] * pick(1, quarter)
-        layer_out[:, columns] = (wide[:, columns] + mixture).astype(BF16)
-    for made in moved:
-        made.wait_recv()
-
-    for head in range(2):
-        grads[head] = lax.dot_general(
-            slab[...], ow_ref[head * 128 : head * 128 + 128, :], NT, preferred_element_type=F32
-        ).astype(BF16)
-    swap = net.copy(grads.at[1 - core], grad_heads.at[own_rows, :], net.sibling)
-    grad_heads[own_rows, :] = grads[core]
-    swap.wait_recv()
-    grad_head = grad_heads[...]
-    delta = jnp.sum(
-        grad_head.astype(F32) * attended_rows[...].astype(F32), axis=1, keepdims=True
-    )
-    dq_rows[...] = jnp.zeros((CHIP_ROWS, HD), F32)
+    def pack_sums(part):
+        def rows_of(quarter, columns):
+            low = part * D + quarter * QUARTER
+            both = [sums[e, 0:ROWS, low : low + QUARTER] for e in range(2)]
+            return jnp.dot(
+                packing(quarter, True),
+                jnp.concatenate(both, axis=0),
+                preferred_element_type=F32,
+            )
+
+        pack(2 + part, rows_of)
+        exchange_slots("returned%d" % part, packed.at[2 + part], returned.at[part])
+
+    def pick(k, part):
+        rows = [
+            jnp.dot(one_hot(found[k], quarter), returned[part], preferred_element_type=F32)
+            for quarter in range(4)
+        ]
+        return jnp.concatenate(rows, axis=1)
+
+    def residual_gradient():
+        wait_for("returned1")
+        wide, inverse = hidden_rows[...], inverse_norm()
+        scaled = gain_ref[...] * (pick(0, 1) + pick(1, 1))
+        cube = inverse * inverse * inverse
+        grad_hidden = go_ref[...].astype(F32) + (
+            inverse * scaled - wide * cube * jnp.mean(wide * scaled, axis=1, keepdims=True)
+        )
+        residual_out[...] = grad_hidden.astype(BF16)
+        keep["slab"] = net.push(lambda peer: residual_out, piece(slab, me))
+        piece(slab, me)[...] = residual_out[...]
+
+    def layer_output():
+        wait_for("returned0")
+        mixture = weight[0] * pick(0, 0) + weight[1] * pick(1, 0)
+        layer_out[...] = (hidden_rows[...] + mixture).astype(BF16)
+
+    def attended_gradient():
+        wait_for("slab")
+        for head in range(2):
+            grads[head] = lax.dot_general(
+                slab[...],
+                ow_ref[head * 128 : head * 128 + 128, :],
+                NT,
+                preferred_element_type=F32,
+            ).astype(BF16)
+        keep["grads"] = [net.copy(grads.at[1 - core], grad_heads.at[own_rows, :], net.sibling)]
+        grad_heads[own_rows, :] = grads[core]
+
+    def row_delta():
+        wait_for("grads")
+        delta_rows[...] = jnp.sum(
+            grad_heads[...].astype(F32) * attended_rows[...].astype(F32), axis=1, keepdims=True
+        )
+        dq_rows[...] = jnp.zeros((CHIP_ROWS, HD), F32)
 
     def back(r):
-        low = softmax[r]
+        low, grad_head = softmax[r], grad_heads[...]
         grad_prob = lax.dot_general(grad_head, kv[r, 256:, :], NT, preferred_element_type=F32)
-        grad_score = (low.astype(F32) * (grad_prob - delta)).astype(BF16)
+        grad_score = (low.astype(F32) * (grad_prob - delta_rows[...])).astype(BF16)
         dq_rows[...] += jnp.dot(grad_score, kv[r, :256, :], preferred_element_type=F32)
         grad_sums[r, :256, :] = (
             lax.dot_general(grad_score, queries[...], TN, preferred_element_type=F32) * SCALE
@@ -584,34 +617,57 @@
             low, grad_head, TN, preferred_element_type=F32
         ).astype(BF16)
 
-    swaps = []
-
     def send_queries():
         dq_other[...] = (dq_rows[other_rows, :] * SCALE).astype(BF16)
-        swaps.append(net.copy(dq_other, pairs.at[0, core], net.sibling))
+        keep["queries"] = [net.copy(dq_other, pairs.at[0, core], net.sibling)]
         pairs[0, core] = (dq_rows[own_rows, :] * SCALE).astype(BF16)
 
     def key_sums(i):
         full = lambda r: grad_sums.at[r, pl.ds(i * 256, 256), :]
         half = lambda r, h: grad_sums.at[r, pl.ds(i * 256 + h * 128, 128), :]
-        return reduce_steps(
-            net,
-            full,
-            half,
-            att_far_y.at[i],
-            att_near_y.at[i],
-            att_far_z.at[i],
-            att_near_z.at[i],
-        )
-
-    backs = [lambda r=r: back(r) for r in range(CHIPS)]
-    run(BACKWARD_ORDER, [key_sums(0), key_sums(1), backs, [send_queries]])
-    swaps.append(net.copy(grad_sums.at[0, other_rows, :], pairs.at[1, core], net.sibling))
-    swaps.append(net.copy(grad_sums.at[0, other_values, :], pairs.at[2, core], net.sibling))
+        buffers = [ref.at[i] for ref in (att_far_y, att_near_y, att_far_z, att_near_z)]
+        return reduce_steps(net, full, half, *buffers)
+
+    for made in exchange:
+        made.wait_recv()
+    run(
+        ORDER,
+        [pair(0, score_block), pair(256, lambda r: None)]
+        + gathers
+        + [compute_steps(e) for e in range(2)]
+        + reduces
+        + [[lambda r=r: back(r) for r in range(CHIPS)], key_sums(0), key_sums(1)]
+        + [[lambda i=i: raise_blocks(i) for i in range(4)]]
+        + [
+            [
+                lambda: score_block(0),
+                send_weights,
+                dispatch_weighted,
+                lambda: unpack(1),
+                attend,
+                project,
+                norm,
+                lambda: unpack(0),
+                lambda: wait_for("weights"),
+                lambda: pack_sums(1),
+                residual_gradient,
+                attended_gradient,
+                row_delta,
+                lambda: pack_sums(0),
+                layer_output,
+                send_queries,
+            ]
+        ],
+    )
+    swaps = [
+        net.copy(grad_sums.at[0, other_rows, :], pairs.at[1, core], net.sibling),
+        net.copy(grad_sums.at[0, other_values, :], pairs.at[2, core], net.sibling),
+    ]
     pairs[1, core] = grad_sums[0, own_rows, :]
     pairs[2, core] = grad_sums[0, own_values, :]
     for made in swaps:
         made.wait_recv()
+    wait_for("queries")
     net.finish()
 
 
@@ -671,8 +727,8 @@
             v(2, 128, HD),
             v(128, D),
             v(128, D),
-            v(128, CHUNK),
-            v(128, CHUNK),
+            v(4, 128, QUARTER),
+            v(2, 128, QUARTER),
             v(2, CHIP_ROWS, 2 * D),
             v(2, CHIP_ROWS, 2 * D),
             v(2, 2, HIDDEN, D),
@@ -687,8 +743,9 @@
             v(4, 2, 4, ROWS, D),
             v(4, 2, ROWS, CHUNK),
             v(4, 4, ROWS, D),
-            v(128, CHUNK),
-            v(128, CHUNK),
+            v(2, 128, QUARTER),
+            pltpu.VMEM((ROWS, D), F32),
+            pltpu.VMEM((CHIP_ROWS, 1), F32),
             v(128, D),
             v(2, 128, HD),
             v(CHIP_ROWS, HD),

time: 164 us -> 150 us (0.915)
  Pallas kernels: 163 us -> 149 us
    pallas_call x1, Pallas kernels: 161 us -> 147 us  [local(): pl.pallas_call(layer_kernel, out_shape=[jax.ShapeDtypeStruct(shape, BF16)...]
where the time goes in v3:
time: 150 us; the launch traced here: 149 us
  Pallas kernels  149 us (99%)
    pallas_call x1, Pallas kernels, local(): pl.pallas_call(layer_kernel, out_shape=[jax.ShapeDtypeStruct(shape, BF16)...  147 us

profile of v3, /device:TPU:1, one launch (start us, length us, event | category | flops | bytes accessed | tf_op | source)
XLA Modules:
  0.0 149.3 jit_solution(13438611012088747937)
XLA Ops:
  0.6 147.0 %shard_map.155 = (bf16[16,2048]{1,0:T(8,128)(2,1)}, bf16[16,2048]{1,0:T(8,128)(2,1)}, bf16[3,2,128,128]{3,2,1,0:T(8,128)(2,1)}) custom-call(bf16[128,256]{1,0:T(8,128)(2,1)} %q_ref.1, bf16[128,256]{1,0:T(8,128)(2,1)} %k_ref.1, bf16[128,256]{1,0:T(8,128)(2,1)} %v_ref.1, bf16[16,2048]{1,0:T(8,128)(2,1)} %residual_ref.1, f32[1,2048]{1,0:T(1,128)} %bitcast.7, ...), custom_call_target="tpu_custom_call" | custom-call | flops 8000000000 | bytes 16777216 | tf_op jit(solution)/shard_map/pallas_call | solution.py:713
  147.6 1.7 %shard_map.156 = (bf16[16,2048]{1,0:T(8,128)(2,1)}, bf16[16,2048]{1,0:T(8,128)(2,1)}, bf16[128,256]{1,0:T(8,128)(2,1)}, bf16[128,256]{1,0:T(8,128)(2,1)}, bf16[128,256]{1,0:T(8,128)(2,1)}) custom-call(bf16[3,2,128,128]{3,2,1,0:T(8,128)(2,1)} %get-tuple-element.8.pairs, bf16[16,2048]{1,0:T(8,128)(2,1)} %get-tuple-element.9.layer_ref, ...), custom_call_target="tpu_custom_call" | custom-call | tf_op jit(solution)/shard_map/pallas_call | solution.py:771

commit v4 on v3

--- a/solution.py
+++ b/solution.py
@@ -26,17 +26,17 @@
 COPIES = 270
 
 ORDER = (
-    0, 1, 16, 258, 17, 2, 257, 18, 3, 4, 20, 19, 5, 21, 259, 80, 6, 256, 8, 7, 22, 24, 48, 264, 9,
-    12, 23, 25, 81, 11, 10, 240, 243, 242, 27, 241, 26, 28, 260, 49, 52, 261, 83, 82, 51, 84, 262,
-    55, 54, 86, 85, 263, 32, 33, 64, 87, 65, 57, 50, 34, 66, 35, 36, 56, 37, 68, 38, 67, 89, 53, 69,
-    40, 58, 91, 41, 39, 70, 43, 44, 42, 97, 96, 59, 60, 99, 73, 98, 105, 106, 92, 88, 90, 104, 107,
-    145, 144, 146, 75, 76, 72, 71, 74, 113, 112, 114, 115, 121, 148, 120, 122, 123, 176, 177, 100,
-    147, 102, 103, 119, 101, 118, 151, 129, 180, 179, 178, 128, 116, 149, 181, 183, 132, 153, 155,
-    152, 154, 185, 182, 184, 186, 187, 150, 135, 130, 117, 161, 156, 157, 131, 188, 189, 265, 160,
-    164, 167, 266, 137, 139, 162, 133, 163, 136, 138, 168, 165, 169, 171, 134, 166, 170, 267, 268,
-    202, 225, 203, 201, 224, 208, 209, 207, 200, 206, 198, 228, 194, 204, 199, 212, 227, 231, 205,
-    197, 226, 215, 211, 172, 140, 141, 173, 210, 269, 196, 213, 195, 233, 229, 193, 232, 234, 235,
-    216, 218, 217, 219, 214, 192, 271, 270, 230, 220, 236, 237, 221,
+    0, 1, 17, 16, 258, 2, 18, 3, 4, 19, 20, 5, 21, 6, 256, 22, 259, 23, 8, 7, 9, 12, 48, 11, 24, 25,
+    80, 27, 28, 10, 243, 240, 241, 242, 26, 260, 81, 261, 49, 51, 82, 84, 52, 83, 262, 85, 54, 50,
+    86, 257, 263, 64, 65, 33, 32, 89, 66, 57, 34, 67, 68, 264, 69, 35, 70, 36, 92, 72, 90, 37, 87,
+    71, 56, 91, 73, 39, 53, 88, 38, 75, 55, 76, 58, 40, 74, 113, 112, 114, 41, 115, 121, 120, 123,
+    122, 177, 59, 60, 179, 176, 43, 44, 42, 97, 96, 99, 98, 107, 180, 105, 104, 106, 145, 144, 116,
+    119, 146, 183, 148, 117, 178, 118, 160, 181, 101, 147, 100, 102, 103, 151, 149, 129, 130, 184,
+    185, 187, 152, 186, 182, 153, 161, 154, 155, 150, 128, 132, 188, 164, 156, 189, 131, 157, 265,
+    133, 162, 167, 165, 135, 266, 137, 163, 169, 136, 138, 168, 134, 166, 139, 171, 170, 267, 268,
+    202, 209, 201, 225, 203, 224, 206, 208, 198, 140, 212, 205, 199, 228, 207, 204, 211, 197, 210,
+    226, 172, 173, 194, 215, 195, 193, 141, 231, 269, 227, 200, 229, 213, 192, 216, 217, 218, 219,
+    196, 232, 271, 234, 233, 235, 230, 270, 214, 220, 221, 236, 237,
 )
 NT = (((1,), (1,)), ((), ()))
 TN = (((0,), (0,)), ((), ()))
@@ -77,6 +77,12 @@
         self.started.append(made)
         return made
 
+    def wait(self, made):
+        for _ in range(3):
+            if len(self.started) > 48:
+                self.started.pop(0).wait_send()
+        made.wait_recv()
+
     def finish(self):
         for made in self.started:
             made.wait_send()
@@ -109,26 +115,26 @@
         state["y1", dz] = net.copy(full(rel(0, dz)), full(rel(1, dz)), net.ym)
 
     def near_z3():
-        state["z3"].wait_recv()
+        net.wait(state["z3"])
         state["h0"] = net.copy(half(rel(0, 3), 0), half(rel(0, 2), 0), net.zp)
         send_y(3)
         seen(rel(0, 3))
 
     def near_z1():
-        state["z1"].wait_recv()
+        net.wait(state["z1"])
         state["h1"] = net.copy(half(rel(0, 1), 1), half(rel(0, 2), 1), net.zm)
         send_y(1)
         seen(rel(0, 1))
 
     def far_z():
-        state["h0"].wait_recv()
-        state["h1"].wait_recv()
+        net.wait(state["h0"])
+        net.wait(state["h1"])
         send_y(2)
         seen(rel(0, 2))
 
     def near_y(dz):
-        state["y3", dz].wait_recv()
-        state["y1", dz].wait_recv()
+        net.wait(state["y3", dz])
+        net.wait(state["y1", dz])
         if dz in (0, 2):
             state["g0", dz] = net.copy(half(rel(3, dz), 0), half(rel(2, dz), 0), net.yp)
             state["g1", dz] = net.copy(half(rel(1, dz), 1), half(rel(2, dz), 1), net.ym)
@@ -136,15 +142,15 @@
         seen(rel(1, dz))
 
     def far_y(dz):
-        state["g0", dz].wait_recv()
-        state["g1", dz].wait_recv()
+        net.wait(state["g0", dz])
+        net.wait(state["g1", dz])
         if dz == 0:
             state["f3"] = net.copy(full(rel(2, 0)), full(rel(2, 3)), net.zp)
             state["f1"] = net.copy(full(rel(2, 0)), full(rel(2, 1)), net.zm)
         seen(rel(2, dz))
 
     def end(dz):
-        state["f%d" % dz].wait_recv()
+        net.wait(state["f%d" % dz])
         seen(rel(2, dz))
 
     return [
@@ -182,42 +188,42 @@
 
     def send_far_y(dz):
         if dz == 0:
-            state["e"].wait_recv()
-            state["f"].wait_recv()
+            net.wait(state["e"])
+            net.wait(state["f"])
             add(full(rel(2, 0)), ze, zf)
         state["a", dz] = net.copy(half(rel(2, dz), 0), ra.at[dz // 2], net.yp)
         state["b", dz] = net.copy(half(rel(2, dz), 1), rb.at[dz // 2], net.ym)
 
     def send_near(dz):
         if dz in (0, 2):
-            state["a", dz].wait_recv()
-            state["b", dz].wait_recv()
+            net.wait(state["a", dz])
+            net.wait(state["b", dz])
             add(half(rel(1, dz), 0), ra.at[dz // 2])
             add(half(rel(3, dz), 1), rb.at[dz // 2])
         state["c", dz] = net.copy(full(rel(1, dz)), rc.at[dz], net.yp)
         state["d", dz] = net.copy(full(rel(3, dz)), rd.at[dz], net.ym)
 
     def collect(dz):
-        state["c", dz].wait_recv()
-        state["d", dz].wait_recv()
+        net.wait(state["c", dz])
+        net.wait(state["d", dz])
         add(full(rel(0, dz)), rc.at[dz], rd.at[dz])
         if dz == 2:
             state["za"] = net.copy(half(rel(0, 2), 0), za, net.zp)
             state["zb"] = net.copy(half(rel(0, 2), 1), zb, net.zm)
 
     def send_z1():
-        state["za"].wait_recv()
+        net.wait(state["za"])
         add(half(rel(0, 1), 0), za)
         state["zc"] = net.copy(full(rel(0, 1)), zc, net.zp)
 
     def send_z3():
-        state["zb"].wait_recv()
+        net.wait(state["zb"])
         add(half(rel(0, 3), 1), zb)
         state["zd"] = net.copy(full(rel(0, 3)), zd, net.zm)
 
     def last():
-        state["zc"].wait_recv()
-        state["zd"].wait_recv()
+        net.wait(state["zc"])
+        net.wait(state["zd"])
         add(full(rel(0, 0)), zc, zd)
 
     return [
@@ -409,7 +415,7 @@
 
     def wait_for(name):
         for made in keep.pop(name):
-            made.wait_recv()
+            net.wait(made)
 
     found = places(ids_ref)
     weight = [column(gw_ref, k) for k in range(2)]
@@ -665,10 +671,9 @@
     ]
     pairs[1, core] = grad_sums[0, own_rows, :]
     pairs[2, core] = grad_sums[0, own_values, :]
-    for made in swaps:
+    net.finish()
+    for made in swaps + keep.pop("queries"):
         made.wait_recv()
-    wait_for("queries")
-    net.finish()
 
 
 def finish_kernel(pairs, layer_ref, residual_ref, layer_out, residual_out, *outs):

time: 150 us -> 146 us (0.973)
  Pallas kernels: 149 us -> 145 us
    pallas_call x1, Pallas kernels: 147 us -> 143 us  [local(): pl.pallas_call(layer_kernel, out_shape=[jax.ShapeDtypeStruct(shape, BF16)...]
where the time goes in v4:
time: 146 us
  Pallas kernels  145 us (99%)
    pallas_call x1, Pallas kernels, local(): pl.pallas_call(layer_kernel, out_shape=[jax.ShapeDtypeStruct(shape, BF16)...  143 us

profile of v4, /device:TPU:1, one launch (start us, length us, event | category | flops | bytes accessed | tf_op | source)
XLA Modules:
  0.0 145.5 jit_solution(13602700868675291367)
XLA Ops:
  0.6 143.2 %shard_map.155 = (bf16[16,2048]{1,0:T(8,128)(2,1)}, bf16[16,2048]{1,0:T(8,128)(2,1)}, bf16[3,2,128,128]{3,2,1,0:T(8,128)(2,1)}) custom-call(bf16[128,256]{1,0:T(8,128)(2,1)} %q_ref.1, bf16[128,256]{1,0:T(8,128)(2,1)} %k_ref.1, bf16[128,256]{1,0:T(8,128)(2,1)} %v_ref.1, bf16[16,2048]{1,0:T(8,128)(2,1)} %residual_ref.1, f32[1,2048]{1,0:T(1,128)} %bitcast.7, ...), custom_call_target="tpu_custom_call" | custom-call | flops 8000000000 | bytes 16777216 | tf_op jit(solution)/shard_map/pallas_call | solution.py:718
  143.8 1.7 %shard_map.156 = (bf16[16,2048]{1,0:T(8,128)(2,1)}, bf16[16,2048]{1,0:T(8,128)(2,1)}, bf16[128,256]{1,0:T(8,128)(2,1)}, bf16[128,256]{1,0:T(8,128)(2,1)}, bf16[128,256]{1,0:T(8,128)(2,1)}) custom-call(bf16[3,2,128,128]{3,2,1,0:T(8,128)(2,1)} %get-tuple-element.8.pairs, bf16[16,2048]{1,0:T(8,128)(2,1)} %get-tuple-element.9.layer_ref, ...), custom_call_target="tpu_custom_call" | custom-call | tf_op jit(solution)/shard_map/pallas_call | solution.py:776

commit v5 on v4

--- a/solution.py
+++ b/solution.py
@@ -23,20 +23,30 @@
 MASKED = -1e30
 SCALE = 1.0 / math.sqrt(HD)
 VMEM_LIMIT = 58 * 1024 * 1024
-COPIES = 270
+COPIES = 488
 
 ORDER = (
-    0, 1, 17, 16, 258, 2, 18, 3, 4, 19, 20, 5, 21, 6, 256, 22, 259, 23, 8, 7, 9, 12, 48, 11, 24, 25,
-    80, 27, 28, 10, 243, 240, 241, 242, 26, 260, 81, 261, 49, 51, 82, 84, 52, 83, 262, 85, 54, 50,
-    86, 257, 263, 64, 65, 33, 32, 89, 66, 57, 34, 67, 68, 264, 69, 35, 70, 36, 92, 72, 90, 37, 87,
-    71, 56, 91, 73, 39, 53, 88, 38, 75, 55, 76, 58, 40, 74, 113, 112, 114, 41, 115, 121, 120, 123,
-    122, 177, 59, 60, 179, 176, 43, 44, 42, 97, 96, 99, 98, 107, 180, 105, 104, 106, 145, 144, 116,
-    119, 146, 183, 148, 117, 178, 118, 160, 181, 101, 147, 100, 102, 103, 151, 149, 129, 130, 184,
-    185, 187, 152, 186, 182, 153, 161, 154, 155, 150, 128, 132, 188, 164, 156, 189, 131, 157, 265,
-    133, 162, 167, 165, 135, 266, 137, 163, 169, 136, 138, 168, 134, 166, 139, 171, 170, 267, 268,
-    202, 209, 201, 225, 203, 224, 206, 208, 198, 140, 212, 205, 199, 228, 207, 204, 211, 197, 210,
-    226, 172, 173, 194, 215, 195, 193, 141, 231, 269, 227, 200, 229, 213, 192, 216, 217, 218, 219,
-    196, 232, 271, 234, 233, 235, 230, 270, 214, 220, 221, 236, 237,
+    0, 1, 16, 17, 33, 49, 448, 48, 32, 465, 2, 18, 3, 4, 50, 20, 449, 19, 451, 34, 452, 460, 51, 52,
+    8, 7, 36, 35, 21, 5, 456, 24, 453, 461, 6, 37, 53, 22, 466, 96, 160, 54, 112, 450, 55, 38, 23,
+    455, 39, 40, 9, 463, 25, 97, 27, 462, 161, 28, 454, 176, 56, 11, 12, 457, 41, 57, 459, 43, 44,
+    10, 26, 458, 435, 434, 433, 432, 59, 58, 60, 42, 467, 164, 99, 163, 100, 468, 162, 113, 177,
+    103, 116, 464, 98, 166, 102, 114, 179, 115, 180, 178, 165, 101, 469, 182, 117, 185, 181, 118,
+    169, 105, 470, 64, 81, 80, 145, 128, 65, 124, 144, 129, 121, 82, 104, 146, 66, 106, 67, 188, 68,
+    83, 84, 122, 186, 131, 132, 69, 167, 85, 130, 187, 70, 86, 147, 148, 119, 72, 183, 171, 123,
+    136, 87, 107, 149, 184, 170, 134, 73, 168, 89, 133, 108, 471, 88, 92, 150, 152, 76, 120, 91,
+    172, 75, 151, 137, 71, 135, 74, 90, 192, 193, 194, 195, 153, 201, 200, 257, 140, 139, 203, 138,
+    256, 155, 202, 272, 273, 259, 156, 154, 209, 208, 210, 260, 211, 219, 218, 337, 276, 217, 216,
+    321, 336, 275, 258, 263, 320, 196, 340, 199, 324, 279, 261, 274, 214, 281, 264, 339, 265, 343,
+    338, 277, 341, 327, 322, 323, 267, 266, 198, 283, 280, 282, 325, 197, 225, 262, 344, 346, 345,
+    347, 278, 328, 330, 329, 331, 342, 215, 213, 326, 240, 212, 304, 242, 305, 224, 290, 289, 268,
+    269, 307, 284, 241, 306, 285, 228, 332, 348, 349, 333, 472, 308, 292, 288, 245, 226, 231, 244,
+    309, 311, 227, 243, 295, 473, 229, 310, 248, 296, 291, 313, 293, 247, 246, 297, 315, 249, 316,
+    312, 314, 298, 294, 299, 474, 233, 300, 251, 235, 232, 234, 250, 230, 252, 475, 362, 401, 385,
+    369, 363, 361, 400, 384, 417, 359, 358, 366, 404, 416, 354, 388, 367, 372, 357, 420, 368, 387,
+    360, 371, 403, 301, 407, 317, 365, 236, 237, 391, 402, 253, 386, 418, 375, 389, 370, 423, 476,
+    353, 421, 419, 355, 409, 411, 408, 410, 393, 405, 373, 392, 395, 394, 356, 377, 364, 379, 390,
+    424, 426, 376, 422, 378, 425, 427, 406, 374, 352, 478, 428, 396, 397, 477, 412, 413, 380, 381,
+    429,
 )
 NT = (((1,), (1,)), ((), ()))
 TN = (((0,), (0,)), ((), ()))
@@ -103,7 +113,7 @@
         return [self.copy(src_of(peer), dst, {"exp": peer}) for peer in self.peers]
 
 
-def gather_steps(net, full, half, seen=lambda r: None):
+def gather_steps(net, full, half):
     state = {}
 
     def send_z():
@@ -118,19 +128,16 @@
         net.wait(state["z3"])
         state["h0"] = net.copy(half(rel(0, 3), 0), half(rel(0, 2), 0), net.zp)
         send_y(3)
-        seen(rel(0, 3))
 
     def near_z1():
         net.wait(state["z1"])
         state["h1"] = net.copy(half(rel(0, 1), 1), half(rel(0, 2), 1), net.zm)
         send_y(1)
-        seen(rel(0, 1))
 
     def far_z():
         net.wait(state["h0"])
         net.wait(state["h1"])
         send_y(2)
-        seen(rel(0, 2))
 
     def near_y(dz):
         net.wait(state["y3", dz])
@@ -138,8 +145,6 @@
         if dz in (0, 2):
             state["g0", dz] = net.copy(half(rel(3, dz), 0), half(rel(2, dz), 0), net.yp)
             state["g1", dz] = net.copy(half(rel(1, dz), 1), half(rel(2, dz), 1), net.ym)
-        seen(rel(3, dz))
-        seen(rel(1, dz))
 
     def far_y(dz):
         net.wait(state["g0", dz])
@@ -147,11 +152,9 @@
         if dz == 0:
             state["f3"] = net.copy(full(rel(2, 0)), full(rel(2, 3)), net.zp)
             state["f1"] = net.copy(full(rel(2, 0)), full(rel(2, 1)), net.zm)
-        seen(rel(2, dz))
 
     def end(dz):
         net.wait(state["f%d" % dz])
-        seen(rel(2, dz))
 
     return [
         send_z,
@@ -403,10 +406,10 @@
 
         row_sum[...] = lax.fori_loop(4 * quarter, 4 * quarter + 4, one, row_sum[...])
 
-    def pair(start, seen):
-        full = lambda r: kv.at[r, pl.ds(start, 256), :]
-        half = lambda r, h: kv.at[r, pl.ds(start + h * 128, 128), :]
-        return gather_steps(net, full, half, seen)
+    def key_block(ref, i):
+        full = lambda r: ref.at[r, pl.ds(i * 128, 128), :]
+        half = lambda r, h: ref.at[r, pl.ds(i * 128 + h * 64, 64), :]
+        return full, half
 
     keep = {}
 
@@ -505,19 +508,19 @@
         pack(0, rows_of)
         exchange_slots("arrived0", packed.at[0], arrived.at[0])
 
-    def block(ref, e, part):
-        full = lambda r: ref.at[e, pl.ds(r * ROWS, ROWS), pl.ds(part * D, D)]
+    def block(ref, i):
+        e, low = i // 4, i % 4 * CHUNK
+        full = lambda r: ref.at[e, pl.ds(r * ROWS, ROWS), pl.ds(low, CHUNK)]
         half = lambda r, h: ref.at[
-            e, pl.ds(r * ROWS, ROWS), pl.ds(part * D + h * CHUNK, CHUNK)
+            e, pl.ds(r * ROWS, ROWS), pl.ds(low + h * QUARTER, QUARTER)
         ]
         return full, half
 
-    parts = [(e, part) for e in range(2) for part in range(2)]
-    gathers = [gather_steps(net, *block(slots, e, part)) for e, part in parts]
+    gathers = [gather_steps(net, *block(slots, i)) for i in range(8)]
     reduces = []
-    for i, (e, part) in enumerate(parts):
+    for i in range(8):
         buffers = [ref.at[i] for ref in (far_y, near_y, far_z, near_z)]
-        reduces.append(reduce_steps(net, *block(sums, e, part), *buffers))
+        reduces.append(reduce_steps(net, *block(sums, i), *buffers))
 
     def compute_steps(e):
         def enter(half):
@@ -629,24 +632,23 @@
         pairs[0, core] = (dq_rows[own_rows, :] * SCALE).astype(BF16)
 
     def key_sums(i):
-        full = lambda r: grad_sums.at[r, pl.ds(i * 256, 256), :]
-        half = lambda r, h: grad_sums.at[r, pl.ds(i * 256 + h * 128, 128), :]
         buffers = [ref.at[i] for ref in (att_far_y, att_near_y, att_far_z, att_near_z)]
-        return reduce_steps(net, full, half, *buffers)
+        return reduce_steps(net, *key_block(grad_sums, i), *buffers)
 
     for made in exchange:
         made.wait_recv()
     run(
         ORDER,
-        [pair(0, score_block), pair(256, lambda r: None)]
+        [gather_steps(net, *key_block(kv, i)) for i in range(4)]
         + gathers
         + [compute_steps(e) for e in range(2)]
         + reduces
-        + [[lambda r=r: back(r) for r in range(CHIPS)], key_sums(0), key_sums(1)]
+        + [[lambda r=r: back(r) for r in range(CHIPS)]]
+        + [key_sums(i) for i in range(4)]
         + [[lambda i=i: raise_blocks(i) for i in range(4)]]
+        + [[lambda r=r: score_block(r) for r in range(CHIPS)]]
         + [
             [
-                lambda: score_block(0),
                 send_weights,
                 dispatch_weighted,
                 lambda: unpack(1),
@@ -744,10 +746,10 @@
             v(2, 2, CHIP_ROWS, HIDDEN),
             v(2, 2, CHIP_ROWS, HIDDEN),
             v(2, 2, CHIP_ROWS, HIDDEN),
-            v(4, 2, 2, ROWS, CHUNK),
-            v(4, 2, 4, ROWS, D),
-            v(4, 2, ROWS, CHUNK),
-            v(4, 4, ROWS, D),
+            v(8, 2, 2, ROWS, QUARTER),
+            v(8, 2, 4, ROWS, CHUNK),
+            v(8, 2, ROWS, QUARTER),
+            v(8, 4, ROWS, CHUNK),
             v(2, 128, QUARTER),
             pltpu.VMEM((ROWS, D), F32),
             pltpu.VMEM((CHIP_ROWS, 1), F32),
@@ -757,10 +759,10 @@
             v(CHIPS, 512, HD),
             pltpu.VMEM((CHIP_ROWS, HD), F32),
             v(128, HD),
-            v(2, 2, 2, 128, HD),
-            v(2, 2, 4, 256, HD),
-            v(2, 2, 128, HD),
-            v(2, 4, 256, HD),
+            v(4, 2, 2, 64, HD),
+            v(4, 2, 4, 128, HD),
+            v(4, 2, 64, HD),
+            v(4, 4, 128, HD),
             pltpu.SemaphoreType.DMA((4,)),
             pltpu.SemaphoreType.DMA((COPIES,)),
             pltpu.SemaphoreType.DMA((COPIES,)),

time: 146 us -> 148 us (1.014)
  Pallas kernels: 145 us -> 147 us
    pallas_call x1, Pallas kernels: 143 us -> 145 us  [local(): pl.pallas_call(layer_kernel, out_shape=[jax.ShapeDtypeStruct(shape, BF16)...]
where the time goes in v5:
time: 148 us
  Pallas kernels  147 us (99%)
    pallas_call x1, Pallas kernels, local(): pl.pallas_call(layer_kernel, out_shape=[jax.ShapeDtypeStruct(shape, BF16)...  145 us

profile of v5, /device:TPU:1, one launch (start us, length us, event | category | flops | bytes accessed | tf_op | source)
XLA Modules:
  0.0 147.7 jit_solution(5642749584286005084)
XLA Ops:
  0.6 145.4 %shard_map.155 = (bf16[16,2048]{1,0:T(8,128)(2,1)}, bf16[16,2048]{1,0:T(8,128)(2,1)}, bf16[3,2,128,128]{3,2,1,0:T(8,128)(2,1)}) custom-call(bf16[128,256]{1,0:T(8,128)(2,1)} %q_ref.1, bf16[128,256]{1,0:T(8,128)(2,1)} %k_ref.1, bf16[128,256]{1,0:T(8,128)(2,1)} %v_ref.1, bf16[16,2048]{1,0:T(8,128)(2,1)} %residual_ref.1, f32[1,2048]{1,0:T(1,128)} %bitcast.7, ...), custom_call_target="tpu_custom_call" | custom-call | flops 8000000000 | bytes 16777216 | tf_op jit(solution)/shard_map/pallas_call | solution.py:720
  146.0 1.7 %shard_map.156 = (bf16[16,2048]{1,0:T(8,128)(2,1)}, bf16[16,2048]{1,0:T(8,128)(2,1)}, bf16[128,256]{1,0:T(8,128)(2,1)}, bf16[128,256]{1,0:T(8,128)(2,1)}, bf16[128,256]{1,0:T(8,128)(2,1)}) custom-call(bf16[3,2,128,128]{3,2,1,0:T(8,128)(2,1)} %get-tuple-element.8.pairs, bf16[16,2048]{1,0:T(8,128)(2,1)} %get-tuple-element.9.layer_ref, ...), custom_call_target="tpu_custom_call" | custom-call | tf_op jit(solution)/shard_map/pallas_call | solution.py:778
